TPU v7x, 32 devices: a whole 2x2x4 slice. The times are simulated.
32 devices in a mesh: wide: 16 (over z, y, x), narrow: 2 (over core).
Axes of the slice: x: 2, y: 2, z: 4, core: 2. Of those that a mesh axis runs over, the one named last changes fastest.
Arguments:
- load: float32 [2048, 512], P(('wide', 'narrow')), may hold values from -48 to 48
- geom: bfloat16 [7, 2048, 512], P(None, ('wide', 'narrow')), may hold values from -0.15 to 3, as said below
- element_order: int32 [16, 2, 64], P('wide', 'narrow'), may hold values from 0 to 63, each once within a row
Outputs:
- solution: float32 [2048, 512], P(('wide', 'narrow'))
- residual: float32 [2048, 512], P(('wide', 'narrow'))
Inputs may be any that keep to these rules, and one draw needn't show every extreme that they name: `geom`: at every point G0, G1, G2 and G6 are positive and |G3|, |G4|, |G5| stay below 0.15. `element_order`: each device's list names each of its 64 block positions exactly once.
All inputs are finite; a program needn't handle non-finite values.
Results may differ from a plain program's by a relative error of at most 0.02.
Values sent between devices are 32-bit elements; how exact they have to be, the bound alone decides.
A program may use at most 64 MiB of HBM per device.

v0:
```python
import jax
import jax.numpy as jnp
import numpy as np
from jax import lax
from jax.sharding import PartitionSpec as P

EZ = 1
EA = 4
ER = 16
CHEB = 3
ITERS = 2
E_DEV = 64


interval_low = 0.03
interval_high = 1.0


def with_halo(cells, sides, width):
    for axis, dim in sides:
        count = lax.axis_size(axis)
        head = lax.slice_in_dim(cells, 0, width, axis=dim)
        tail = lax.slice_in_dim(cells, cells.shape[dim] - width, cells.shape[dim], axis=dim)
        cells = jnp.concatenate(
            [
                lax.ppermute(tail, axis, [(i, (i + 1) % count) for i in range(count)]),
                cells,
                lax.ppermute(head, axis, [((i + 1) % count, i) for i in range(count)]),
            ],
            axis=dim,
        )
    return cells


def legendre_seven(point):
    before = 1.0
    current = point
    for degree in range(1, 7):
        after = ((2.0 * degree + 1.0) * point * current - degree * before) / (degree + 1.0)
        before = current
        current = after
    return current


def gll_derivative():
    points = 8
    inner_nodes = [
        -0.8717401485096066,
        -0.5917001814331423,
        -0.2092992179024789,
        0.2092992179024789,
        0.5917001814331423,
        0.8717401485096066,
    ]
    nodes = [-1.0] + inner_nodes + [1.0]
    values_at = [legendre_seven(node) for node in nodes]
    matrix = np.zeros((points, points))
    for source in range(points):
        for target in range(points):
            if source != target:
                matrix[source, target] = values_at[source] / (
                    values_at[target] * (nodes[source] - nodes[target])
                )
    matrix[0, 0] = -(points - 1) * points / 4.0
    matrix[points - 1, points - 1] = (points - 1) * points / 4.0
    return matrix


def radial_apply(field, radial_matrix):
    flat = field.reshape(-1, field.shape[-1])
    result = jnp.dot(
        flat, radial_matrix, precision=lax.Precision.HIGHEST, preferred_element_type=jnp.float32
    )
    return result.reshape(field.shape)


def gradients(field, derivative, radial_matrix):
    pipe_len, cycle_len, radial_len = field.shape
    blocks = field.reshape(pipe_len // 8, 8, cycle_len // 8, 8, radial_len)
    highest = lax.Precision.HIGHEST
    grad_z = jnp.einsum("im,pmqjr->piqjr", derivative, blocks, precision=highest)
    grad_a = jnp.einsum("jm,piqmr->piqjr", derivative, blocks, precision=highest)
    grad_r = radial_apply(field, radial_matrix.T)
    return (grad_z.reshape(field.shape), grad_a.reshape(field.shape), grad_r)


def divergence(flux_z, flux_a, flux_r, derivative, radial_matrix):
    pipe_len, cycle_len, radial_len = flux_z.shape
    shape5 = (pipe_len // 8, 8, cycle_len // 8, 8, radial_len)
    highest = lax.Precision.HIGHEST
    part_z = jnp.einsum(
        "mi,pmqjr->piqjr", derivative, flux_z.reshape(shape5), precision=highest
    ).reshape(flux_z.shape)
    part_a = jnp.einsum(
        "mj,piqmr->piqjr", derivative, flux_a.reshape(shape5), precision=highest
    ).reshape(flux_z.shape)
    part_r = radial_apply(flux_r, radial_matrix)
    return part_z + part_a + part_r


def element_apply(field, metric, derivative, radial_matrix):
    grad_z, grad_a, grad_r = gradients(field, derivative, radial_matrix)
    g_zz = metric[0].astype(jnp.float32)
    g_aa = metric[1].astype(jnp.float32)
    g_rr = metric[2].astype(jnp.float32)
    g_za = metric[3].astype(jnp.float32)
    g_zr = metric[4].astype(jnp.float32)
    g_ar = metric[5].astype(jnp.float32)
    flux_z = g_zz * grad_z + g_za * grad_a + g_zr * grad_r
    flux_a = g_za * grad_z + g_aa * grad_a + g_ar * grad_r
    flux_r = g_zr * grad_z + g_ar * grad_a + g_rr * grad_r
    return (
        divergence(flux_z, flux_a, flux_r, derivative, radial_matrix)
        + metric[6].astype(jnp.float32) * field
    )


def element_bound(metric, derivative, radial_count):
    pipe_len, cycle_len, radial_len = metric.shape[1:]
    absolute = jnp.abs(derivative)
    radial_absolute = jnp.kron(jnp.eye(radial_count, dtype=jnp.float32), absolute)
    row_total = jnp.sum(absolute, axis=1)
    q_z = jnp.tile(row_total, pipe_len // 8)[:, None, None]
    q_a = jnp.tile(row_total, cycle_len // 8)[None, :, None]
    q_r = jnp.tile(row_total, radial_len // 8)[None, None, :]
    g_abs = jnp.abs(metric.astype(jnp.float32))
    h_z = g_abs[0] * q_z + g_abs[3] * q_a + g_abs[4] * q_r
    h_a = g_abs[3] * q_z + g_abs[1] * q_a + g_abs[5] * q_r
    h_r = g_abs[4] * q_z + g_abs[5] * q_a + g_abs[2] * q_r
    return divergence(h_z, h_a, h_r, absolute, radial_absolute) + g_abs[6]


def pair_sum(padded, axis):
    length = padded.shape[axis] - 2
    core = lax.slice_in_dim(padded, 1, length + 1, axis=axis)
    upper = lax.slice_in_dim(padded, 2, length + 2, axis=axis)
    lower = lax.slice_in_dim(padded, 0, length, axis=axis)
    node = lax.broadcasted_iota(jnp.int32, core.shape, axis) % 8
    return core + jnp.where(node == 7, upper, 0.0) + jnp.where(node == 0, lower, 0.0)


def point_weight(pipe_len, cycle_len, radial_len):
    one = jnp.float32(1.0)
    two = jnp.float32(2.0)
    pipe_node = jnp.arange(pipe_len) % 8
    cycle_node = jnp.arange(cycle_len) % 8
    radial_index = jnp.arange(radial_len)
    radial_node = radial_index % 8
    count_z = jnp.where((pipe_node == 0) | (pipe_node == 7), two, one)
    count_a = jnp.where((cycle_node == 0) | (cycle_node == 7), two, one)
    inside = (radial_index > 0) & (radial_index < radial_len - 1)
    count_r = jnp.where(((radial_node == 0) | (radial_node == 7)) & inside, two, one)
    return one / (count_z[:, None, None] * count_a[None, :, None] * count_r[None, None, :])


def assemble(stacked):
    padded = with_halo(stacked, (("wide", 1), ("narrow", 2)), 1)
    merged = pair_sum(pair_sum(padded, 1), 2)
    radial = jnp.pad(merged, ((0, 0), (0, 0), (0, 0), (1, 1)))
    return pair_sum(radial, 3)


def local(load, geom, element_order):
    derivative = jnp.asarray(gll_derivative(), dtype=jnp.float32)
    radial_matrix = jnp.kron(jnp.eye(ER, dtype=jnp.float32), derivative)
    order_flat = element_order.reshape(-1)
    inverse = jnp.argsort(order_flat)
    pipe_len = EZ * 8
    cycle_len = EA * 8
    radial_len = ER * 8
    placed = jnp.take(load, inverse, axis=0)
    load_grid = (
        placed.reshape(EZ, EA, ER, 8, 8, 8)
        .transpose(0, 3, 1, 4, 2, 5)
        .reshape(pipe_len, cycle_len, radial_len)
    )
    placed_geom = jnp.take(geom, inverse, axis=1)
    metric = placed_geom.reshape(7, EZ, EA, ER, 8, 8, 8).transpose(0, 1, 4, 2, 5, 3, 6)
    metric = metric.reshape(7, pipe_len, cycle_len, radial_len)
    local_bound = element_bound(metric, derivative, ER)
    assembled = assemble(jnp.stack([load_grid, local_bound]))
    grid_residual = assembled[0]
    bound_inverse = 1.0 / assembled[1]
    weight = point_weight(pipe_len, cycle_len, radial_len)

    def operator(field):
        return assemble(element_apply(field, metric, derivative, radial_matrix)[None])[0]

    def inner(first_field, second_field):
        return jnp.sum(first_field * second_field * weight)

    center = (interval_high + interval_low) / 2.0
    half_width = (interval_high - interval_low) / 2.0
    sigma_ratio = center / half_width
    grid_solution = jnp.zeros_like(grid_residual)
    direction = grid_residual
    previous = jnp.float32(1.0)
    step_size = jnp.float32(1.0)
    for iteration in range(ITERS):
        rho_now = 1.0 / sigma_ratio
        update = grid_residual * bound_inverse / center
        result = update
        for degree_step in range(CHEB - 1):
            rho_next = 1.0 / (2.0 * sigma_ratio - rho_now)
            update = rho_next * rho_now * update + 2.0 * rho_next / half_width * bound_inverse * (
                grid_residual - operator(result)
            )
            result = result + update
            rho_now = rho_next
        precond_norm = lax.psum(inner(grid_residual, result), ("wide", "narrow"))
        if iteration == 0:
            direction = result
        else:
            direction = result + precond_norm / previous * direction
        image = operator(direction)
        step_size = precond_norm / lax.psum(inner(direction, image), ("wide", "narrow"))
        grid_solution = grid_solution + step_size * direction
        grid_residual = grid_residual - step_size * image
        previous = precond_norm

    def read_back(grid_field):
        rows = (
            grid_field.reshape(EZ, 8, EA, 8, ER, 8).transpose(0, 2, 4, 1, 3, 5).reshape(E_DEV, 512)
        )
        return jnp.take(rows, order_flat, axis=0)

    return (read_back(grid_solution), read_back(grid_residual))


def solution(mesh):
    placed = (
        P(("wide", "narrow"), None),
        P(None, ("wide", "narrow"), None),
        P("wide", "narrow", None),
    )
    return jax.shard_map(
        local,
        mesh=mesh,
        in_specs=placed,
        out_specs=(P(("wide", "narrow"), None), P(("wide", "narrow"), None)),
        check_vma=False,
    )
```

profile of v0, /device:TPU:0, one launch (start us, length us, event | category | flops | bytes accessed | tf_op | source)
XLA Modules:
  0.0 316.8 jit_solution(1133885493075158302)
XLA Ops:
  0.7 2.7 sort.17
  3.4 1.9 gather_fusion
  5.8 3.2 %gather.10 = bf16[7,1,4,16,8,8,8]{3,2,6,5,4,0,1:T(4,128)(2,1)} reshape(bf16[7,64,512]{1,2,0:T(8,128)(2,1)S(1)} %copy.141) | data formatting | bytes 917504 | tf_op jit(solution)/shard_map/jit(_take)/gather | solution.py:177
  9.1 5.3 %convert_abs_fusion = (f32[7,1,8,4,8,16,8]{5,6,4,3,2,1,0:T(8,128)S(1)}, bf16[7,1,8,4,8,16,8]{5,6,4,3,2,1,0:T(8,128)(2,1)}) fusion(bf16[7,1,4,16,8,8,8]{3,2,6,5,4,0,1:T(4,128)(2,1)} %gather.10, pred[4,16]{1,0:T(4,128)(4,1)S(1)} %broadcast_in_dim.130), kind=kLoop, calls=%fused_computation.4 | loop fusion | flops 688128 | bytes 1835072 | tf_op jit(solution)/shard_map/abs | solution.py:126
  14.4 3.1 fusion.321
  28.3 1.9 copy.143
  36.0 2.0 slice.373
  38.1 1.9 copy.155
  51.2 3.0 collective-permute-start
  54.2 4.1 %collective-permute-start.1 = (f32[2,1,32,128]{3,2,1,0:T(8,128)S(1)}, f32[2,1,32,128]{3,2,1,0:T(8,128)S(1)}, u32[]{:S(2)}, u32[]{:S(2)}) collective-permute-start(f32[2,1,32,128]{3,2,1,0:T(8,128)S(1)} %get-tuple-element.46), channel_id=1, source_target_pairs={{2,0},{4,2},{6,4},{8,6},{10,8},{12,10},{14,12},{16,14},{18,16},{20... | collective-permute-start | bytes 98312 | tf_op jit(solution)/shard_map/ppermute | solution.py:28
  58.3 5.2 %slice_convert_fusion.1 = (f32[1,1,8,4,8,16,8]{5,6,4,3,2,1,0:T(8,128)}, f32[1,1,8,4,8,16,8]{5,6,4,3,2,1,0:T(8,128)}, f32[1,1,8,4,8,16,8]{5,6,4,3,2,1,0:T(8,128)}...) fusion(bf16[7,1,8,4,8,16,8]{5,6,4,3,2,1,0:T(8,128)(2,1)} %get-t, ...), kind=kLoop, calls=%fused_computation.53 | loop fusion | flops 229376 | bytes 1376256 | tf_op jit(solution)/shard_map/convert_element_type | solution.py:105
  64.7 1.9 copy.159
  87.8 5.6 %collective-permute-start.5 = (f32[1,1,32,128]{3,2,1,0:T(8,128)S(1)}, f32[1,1,32,128]{3,2,1,0:T(8,128)S(1)}, u32[]{:S(2)}, u32[]{:S(2)}) collective-permute-start(f32[1,1,32,128]{3,2,1,0:T(8,128)S(1)} %get-tuple-element.70), channel_id=1, source_target_pairs={{2,0},{4,2},{6,4},{8,6},{10,8},{12,10},{14,12},{16,14},{18,16},{20... | collective-permute-start | bytes 49160 | tf_op jit(solution)/shard_map/ppermute | solution.py:28
  98.9 5.7 %collective-permute-start.9 = (f32[1,1,32,128]{3,2,1,0:T(8,128)S(1)}, f32[1,1,32,128]{3,2,1,0:T(8,128)S(1)}, u32[]{:S(2)}, u32[]{:S(2)}) collective-permute-start(f32[1,1,32,128]{3,2,1,0:T(8,128)S(1)} %get-tuple-element.68), channel_id=1, source_target_pairs={{2,0},{4,2},{6,4},{8,6},{10,8},{12,10},{14,12},{16,14},{18,16},{20... | collective-permute-start | bytes 49160 | tf_op jit(solution)/shard_map/ppermute | solution.py:28
  110.2 5.7 %collective-permute-start.13 = (f32[1,1,32,128]{3,2,1,0:T(8,128)S(1)}, f32[1,1,32,128]{3,2,1,0:T(8,128)S(1)}, u32[]{:S(2)}, u32[]{:S(2)}) collective-permute-start(f32[1,1,32,128]{3,2,1,0:T(8,128)S(1)} %get-tuple-element.66), channel_id=1, source_target_pairs={{2,0},{4,2},{6,4},{8,6},{10,8},{12,10},{14,12},{16,14},{18,16},{20... | collective-permute-start | bytes 49160 | tf_op jit(solution)/shard_map/ppermute | solution.py:28
  120.1 40.4 %all-reduce.7 = (f32[]{:T(128)}, f32[]{:T(128)}) all-reduce(f32[]{:T(128)} %get-tuple-element.6, f32[]{:T(128)} %get-tuple-element.5), channel_id=1, replica_groups=mesh['wide'=16,'narrow'=2] {'wide','narrow'}, use_global_device_ids=true, to_apply=%region_3.5 | all-reduce | flops 2 | bytes 16 | tf_op jit(solution)/shard_map/psum | solution.py:210
  163.8 2.3 collective-permute-start.16
  166.2 3.3 %collective-permute-start.17 = (f32[1,1,32,128]{3,2,1,0:T(8,128)S(1)}, f32[1,1,32,128]{3,2,1,0:T(8,128)S(1)}, u32[]{:S(2)}, u32[]{:S(2)}) collective-permute-start(f32[1,1,32,128]{3,2,1,0:T(8,128)S(1)} %get-tuple-element.64), channel_id=1, source_target_pairs={{2,0},{4,2},{6,4},{8,6},{10,8},{12,10},{14,12},{16,14},{18,16},{20... | collective-permute-start | bytes 49160 | tf_op jit(solution)/shard_map/ppermute | solution.py:28
  176.5 4.4 %collective-permute-start.21 = (f32[1,1,32,128]{3,2,1,0:T(8,128)S(1)}, f32[1,1,32,128]{3,2,1,0:T(8,128)S(1)}, u32[]{:S(2)}, u32[]{:S(2)}) collective-permute-start(f32[1,1,32,128]{3,2,1,0:T(8,128)S(1)} %get-tuple-element.62), channel_id=1, source_target_pairs={{2,0},{4,2},{6,4},{8,6},{10,8},{12,10},{14,12},{16,14},{18,16},{20... | collective-permute-start | bytes 49160 | tf_op jit(solution)/shard_map/ppermute | solution.py:28
  185.0 40.5 %psum.30 = f32[]{:T(128)} all-reduce(f32[]{:T(128)} %get-tuple-element.11), channel_id=1, replica_groups=mesh['wide'=16,'narrow'=2] {'wide','narrow'}, use_global_device_ids=true, to_apply=%region_7.9 | all-reduce | flops 1 | bytes 8 | tf_op jit(solution)/shard_map/psum | solution.py:210
  229.1 2.3 collective-permute-start.24
  231.4 3.3 %collective-permute-start.25 = (f32[1,1,32,128]{3,2,1,0:T(8,128)S(1)}, f32[1,1,32,128]{3,2,1,0:T(8,128)S(1)}, u32[]{:S(2)}, u32[]{:S(2)}) collective-permute-start(f32[1,1,32,128]{3,2,1,0:T(8,128)S(1)} %get-tuple-element.60), channel_id=1, source_target_pairs={{2,0},{4,2},{6,4},{8,6},{10,8},{12,10},{14,12},{16,14},{18,16},{20... | collective-permute-start | bytes 49160 | tf_op jit(solution)/shard_map/ppermute | solution.py:28
  238.2 2.5 squeeze.59
  240.7 2.4 squeeze.120
  243.2 2.5 squeeze.121
  245.7 2.5 mul.1102
  248.2 2.4 squeeze.127
  250.7 2.6 squeeze.128
  254.4 40.5 %psum.31 = f32[]{:T(128)} all-reduce(f32[]{:T(128)} %get-tuple-element.9), channel_id=1, replica_groups=mesh['wide'=16,'narrow'=2] {'wide','narrow'}, use_global_device_ids=true, to_apply=%region_9.11 | all-reduce | flops 1 | bytes 8 | tf_op jit(solution)/shard_map/psum | solution.py:216
  296.3 2.4 mul.1113
  298.7 7.7 %subtract_bitcast_fusion = (f32[1,4,16,8,8,8]{5,2,4,1,3,0:T(8,128)}, f32[1,4,16,8,8,8]{5,2,4,1,3,0:T(8,128)}) fusion(f32[1,8,4,8,16,8]{5,4,3,2,1,0:T(8,128)} %mul.1113, f32[1,8,4,8,16,8]{5,4,3,2,1,0:T(8,128)} %squeeze.59, f32[1,8,4,8,16,8]{5,4,3,2,1,0:T(8,128)} %mul.1102, f32[]{:T(128)S(6)} %div.110, f32[1,8,4,8,16,8]{5,4,3,2,1,0:T(8,128)} %squeeze.128, ...), kind=kLoop, calls=%fused_computation.7 | loop fusion | flops 1081344 | bytes 1310732 | tf_op jit(solution)/shard_map/transpose | solution.py:223
  306.4 2.8 copy.217
  (300 shorter events, 92.3 us)
Async XLA Ops:
  51.2 12.4 %collective-permute-start = (f32[2,1,32,128]{3,2,1,0:T(8,128)S(1)}, f32[2,1,32,128]{3,2,1,0:T(8,128)S(1)}, u32[]{:S(2)}, u32[]{:S(2)}) collective-permute-start(f32[2,1,32,128]{3,2,1,0:T(8,128)S(1)} %get-tuple-element.45), channel_id=1, source_target_pairs={{0,2},{2,4},{4,6},{6,8},{8,10},{10,12},{12,14},{14,16},{16,18},{18... | collective-permute-start | bytes 98312 | tf_op jit(solution)/shard_map/ppermute | solution.py:26
  54.2 9.4 %collective-permute-start.1 = (f32[2,1,32,128]{3,2,1,0:T(8,128)S(1)}, f32[2,1,32,128]{3,2,1,0:T(8,128)S(1)}, u32[]{:S(2)}, u32[]{:S(2)}) collective-permute-start(f32[2,1,32,128]{3,2,1,0:T(8,128)S(1)} %get-tuple-element.46), channel_id=1, source_target_pairs={{2,0},{4,2},{6,4},{8,6},{10,8},{12,10},{14,12},{16,14},{18,16},{20... | collective-permute-start | bytes 98312 | tf_op jit(solution)/shard_map/ppermute | solution.py:28
  58.2 114.5 %copy-start.32 = (s32[8]{0:T(128)}, s32[8]{0:T(128)S(1)}, u32[]{:S(2)}) copy-start(s32[8]{0:T(128)S(1)} %get-tuple-element.76) | copy-start | bytes 100
  58.2 114.5 %copy-start.35 = (pred[8]{0:T(512)(128)(4,1)}, pred[8]{0:T(512)(128)(4,1)S(1)}, u32[]{:S(2)}) copy-start(pred[8]{0:T(512)(128)(4,1)S(1)} %compare_and_fusion.4) | copy-start | bytes 28
  63.6 21.4 %collective-permute-start.2 = (f32[2,10,1,128]{3,2,1,0:T(1,128)S(1)}, f32[2,10,1,128]{3,2,1,0:T(1,128)S(1)}, u32[]{:S(2)}, u32[]{:S(2)}) collective-permute-start(f32[2,10,1,128]{3,2,1,0:T(1,128)S(1)} %get-tuple-element.41), channel_id=1, source_target_pairs={{0,1},{1,0},{2,3},{3,2},{4,5},{5,4},{6,7},{7,6},{8,9},{9,8},{10,11... | collective-permute-start | bytes 30728 | tf_op jit(solution)/shard_map/ppermute | solution.py:26
  63.7 21.3 %collective-permute-start.3 = (f32[2,10,1,128]{3,2,1,0:T(1,128)S(1)}, f32[2,10,1,128]{3,2,1,0:T(1,128)S(1)}, u32[]{:S(2)}, u32[]{:S(2)}) collective-permute-start(f32[2,10,1,128]{3,2,1,0:T(1,128)S(1)} %get-tuple-element.42), channel_id=1, source_target_pairs={{1,0},{0,1},{3,2},{2,3},{5,4},{4,5},{7,6},{6,7},{9,8},{8,9},{11,10... | collective-permute-start | bytes 30728 | tf_op jit(solution)/shard_map/ppermute | solution.py:28
  87.7 7.4 %collective-permute-start.4 = (f32[1,1,32,128]{3,2,1,0:T(8,128)S(1)}, f32[1,1,32,128]{3,2,1,0:T(8,128)S(1)}, u32[]{:S(2)}, u32[]{:S(2)}) collective-permute-start(f32[1,1,32,128]{3,2,1,0:T(8,128)S(1)} %get-tuple-element.69), channel_id=1, source_target_pairs={{0,2},{2,4},{4,6},{6,8},{8,10},{10,12},{12,14},{14,16},{16,18},{18... | collective-permute-start | bytes 49160 | tf_op jit(solution)/shard_map/ppermute | solution.py:26
  87.8 7.3 %collective-permute-start.5 = (f32[1,1,32,128]{3,2,1,0:T(8,128)S(1)}, f32[1,1,32,128]{3,2,1,0:T(8,128)S(1)}, u32[]{:S(2)}, u32[]{:S(2)}) collective-permute-start(f32[1,1,32,128]{3,2,1,0:T(8,128)S(1)} %get-tuple-element.70), channel_id=1, source_target_pairs={{2,0},{4,2},{6,4},{8,6},{10,8},{12,10},{14,12},{16,14},{18,16},{20... | collective-permute-start | bytes 49160 | tf_op jit(solution)/shard_map/ppermute | solution.py:28
  95.1 1.2 collective-permute-start.6
  95.2 1.3 collective-permute-start.7
  98.9 7.4 %collective-permute-start.8 = (f32[1,1,32,128]{3,2,1,0:T(8,128)S(1)}, f32[1,1,32,128]{3,2,1,0:T(8,128)S(1)}, u32[]{:S(2)}, u32[]{:S(2)}) collective-permute-start(f32[1,1,32,128]{3,2,1,0:T(8,128)S(1)} %get-tuple-element.67), channel_id=1, source_target_pairs={{0,2},{2,4},{4,6},{6,8},{8,10},{10,12},{12,14},{14,16},{16,18},{18... | collective-permute-start | bytes 49160 | tf_op jit(solution)/shard_map/ppermute | solution.py:26
  98.9 7.3 %collective-permute-start.9 = (f32[1,1,32,128]{3,2,1,0:T(8,128)S(1)}, f32[1,1,32,128]{3,2,1,0:T(8,128)S(1)}, u32[]{:S(2)}, u32[]{:S(2)}) collective-permute-start(f32[1,1,32,128]{3,2,1,0:T(8,128)S(1)} %get-tuple-element.68), channel_id=1, source_target_pairs={{2,0},{4,2},{6,4},{8,6},{10,8},{12,10},{14,12},{16,14},{18,16},{20... | collective-permute-start | bytes 49160 | tf_op jit(solution)/shard_map/ppermute | solution.py:28
  106.3 1.2 collective-permute-start.10
  106.3 1.3 collective-permute-start.11
  108.1 119.5 %copy-start.12 = (f32[1,8,32,128]{3,2,1,0:T(8,128)}, f32[1,8,32,128]{3,2,1,0:T(8,128)S(1)}, u32[]{:S(2)}) copy-start(f32[1,8,32,128]{3,2,1,0:T(8,128)S(1)} %get-tuple-element.20) | copy-start | bytes 393220
  108.1 120.7 %copy-start.5 = (f32[8,32,128]{2,1,0:T(8,128)}, f32[8,32,128]{2,1,0:T(8,128)S(1)}, u32[]{:S(2)}) copy-start(f32[8,32,128]{2,1,0:T(8,128)S(1)} %get-tuple-element.19) | copy-start | bytes 393220
  110.1 7.5 %collective-permute-start.12 = (f32[1,1,32,128]{3,2,1,0:T(8,128)S(1)}, f32[1,1,32,128]{3,2,1,0:T(8,128)S(1)}, u32[]{:S(2)}, u32[]{:S(2)}) collective-permute-start(f32[1,1,32,128]{3,2,1,0:T(8,128)S(1)} %get-tuple-element.65), channel_id=1, source_target_pairs={{0,2},{2,4},{4,6},{6,8},{8,10},{10,12},{12,14},{14,16},{16,18},{18... | collective-permute-start | bytes 49160 | tf_op jit(solution)/shard_map/ppermute | solution.py:26
  110.2 7.4 %collective-permute-start.13 = (f32[1,1,32,128]{3,2,1,0:T(8,128)S(1)}, f32[1,1,32,128]{3,2,1,0:T(8,128)S(1)}, u32[]{:S(2)}, u32[]{:S(2)}) collective-permute-start(f32[1,1,32,128]{3,2,1,0:T(8,128)S(1)} %get-tuple-element.66), channel_id=1, source_target_pairs={{2,0},{4,2},{6,4},{8,6},{10,8},{12,10},{14,12},{16,14},{18,16},{20... | collective-permute-start | bytes 49160 | tf_op jit(solution)/shard_map/ppermute | solution.py:28
  117.6 1.2 collective-permute-start.14
  117.7 1.3 collective-permute-start.15
  163.8 7.4 %collective-permute-start.16 = (f32[1,1,32,128]{3,2,1,0:T(8,128)S(1)}, f32[1,1,32,128]{3,2,1,0:T(8,128)S(1)}, u32[]{:S(2)}, u32[]{:S(2)}) collective-permute-start(f32[1,1,32,128]{3,2,1,0:T(8,128)S(1)} %get-tuple-element.63), channel_id=1, source_target_pairs={{0,2},{2,4},{4,6},{6,8},{8,10},{10,12},{12,14},{14,16},{16,18},{18... | collective-permute-start | bytes 49160 | tf_op jit(solution)/shard_map/ppermute | solution.py:26
  166.2 5.1 %collective-permute-start.17 = (f32[1,1,32,128]{3,2,1,0:T(8,128)S(1)}, f32[1,1,32,128]{3,2,1,0:T(8,128)S(1)}, u32[]{:S(2)}, u32[]{:S(2)}) collective-permute-start(f32[1,1,32,128]{3,2,1,0:T(8,128)S(1)} %get-tuple-element.64), channel_id=1, source_target_pairs={{2,0},{4,2},{6,4},{8,6},{10,8},{12,10},{14,12},{16,14},{18,16},{20... | collective-permute-start | bytes 49160 | tf_op jit(solution)/shard_map/ppermute | solution.py:28
  171.2 1.2 collective-permute-start.18
  171.3 1.3 collective-permute-start.19
  175.1 7.4 %collective-permute-start.20 = (f32[1,1,32,128]{3,2,1,0:T(8,128)S(1)}, f32[1,1,32,128]{3,2,1,0:T(8,128)S(1)}, u32[]{:S(2)}, u32[]{:S(2)}) collective-permute-start(f32[1,1,32,128]{3,2,1,0:T(8,128)S(1)} %get-tuple-element.61), channel_id=1, source_target_pairs={{0,2},{2,4},{4,6},{6,8},{8,10},{10,12},{12,14},{14,16},{16,18},{18... | collective-permute-start | bytes 49160 | tf_op jit(solution)/shard_map/ppermute | solution.py:26
  176.5 6.0 %collective-permute-start.21 = (f32[1,1,32,128]{3,2,1,0:T(8,128)S(1)}, f32[1,1,32,128]{3,2,1,0:T(8,128)S(1)}, u32[]{:S(2)}, u32[]{:S(2)}) collective-permute-start(f32[1,1,32,128]{3,2,1,0:T(8,128)S(1)} %get-tuple-element.62), channel_id=1, source_target_pairs={{2,0},{4,2},{6,4},{8,6},{10,8},{12,10},{14,12},{16,14},{18,16},{20... | collective-permute-start | bytes 49160 | tf_op jit(solution)/shard_map/ppermute | solution.py:28
  182.5 1.2 collective-permute-start.22
  182.6 1.3 collective-permute-start.23
  229.1 7.4 %collective-permute-start.24 = (f32[1,1,32,128]{3,2,1,0:T(8,128)S(1)}, f32[1,1,32,128]{3,2,1,0:T(8,128)S(1)}, u32[]{:S(2)}, u32[]{:S(2)}) collective-permute-start(f32[1,1,32,128]{3,2,1,0:T(8,128)S(1)} %get-tuple-element.59), channel_id=1, source_target_pairs={{0,2},{2,4},{4,6},{6,8},{8,10},{10,12},{12,14},{14,16},{16,18},{18... | collective-permute-start | bytes 49160 | tf_op jit(solution)/shard_map/ppermute | solution.py:26
  231.4 5.1 %collective-permute-start.25 = (f32[1,1,32,128]{3,2,1,0:T(8,128)S(1)}, f32[1,1,32,128]{3,2,1,0:T(8,128)S(1)}, u32[]{:S(2)}, u32[]{:S(2)}) collective-permute-start(f32[1,1,32,128]{3,2,1,0:T(8,128)S(1)} %get-tuple-element.60), channel_id=1, source_target_pairs={{2,0},{4,2},{6,4},{8,6},{10,8},{12,10},{14,12},{16,14},{18,16},{20... | collective-permute-start | bytes 49160 | tf_op jit(solution)/shard_map/ppermute | solution.py:28
  236.5 16.8 %collective-permute-start.26 = (f32[1,10,1,128]{3,2,1,0:T(1,128)S(1)}, f32[1,10,1,128]{3,2,1,0:T(1,128)S(1)}, u32[]{:S(2)}, u32[]{:S(2)}) collective-permute-start(f32[1,10,1,128]{3,2,1,0:T(1,128)S(1)} %get-tuple-element.47), channel_id=1, source_target_pairs={{0,1},{1,0},{2,3},{3,2},{4,5},{5,4},{6,7},{7,6},{8,9},{9,8},{10,11... | collective-permute-start | bytes 15368 | tf_op jit(solution)/shard_map/ppermute | solution.py:26
  236.6 16.7 %collective-permute-start.27 = (f32[1,10,1,128]{3,2,1,0:T(1,128)S(1)}, f32[1,10,1,128]{3,2,1,0:T(1,128)S(1)}, u32[]{:S(2)}, u32[]{:S(2)}) collective-permute-start(f32[1,10,1,128]{3,2,1,0:T(1,128)S(1)} %get-tuple-element.48), channel_id=1, source_target_pairs={{1,0},{0,1},{3,2},{2,3},{5,4},{4,5},{7,6},{6,7},{9,8},{8,9},{11,10... | collective-permute-start | bytes 15368 | tf_op jit(solution)/shard_map/ppermute | solution.py:28
  (41 other events, 771.0 us)
where the time goes:
time: 320 us; the launch traced here: 317 us
  blocking collectives  121 us (38%)
  local copies, waits for them, and re-layouts  87.8 us (27%)
  starting transfers between devices  45.3 us (14%)
  other arithmetic  29.5 us (9%)
  waiting for transfers between devices  13.6 us (4%)
  matrix products  12.8 us (4%)
  between operations  6.45 us (2%)
    psum x2, blocking collectives, local(): precond_norm = lax.psum(inner(grid_residual, result), ('wide', 'narrow'))  80.8 us
    psum x1, blocking collectives, local(): lax.psum(inner(direction, image), ('wide', 'narrow'))  40.5 us
    ppermute x14, starting transfers between devices, with_halo(): lax.ppermute(head, axis, [((i + 1) % count, i) for i in range(count)])  35.6 us
    ppermute x14, waiting for transfers between devices, with_halo(): lax.ppermute(tail, axis, [(i, (i + 1) % count) for i in range(count)])  12.8 us
    squeeze x4, local copies, waits for them, and re-layouts, operator(): assemble(element_apply(field, metric, derivative, radial_matrix)[None])[0]  9.94 us
    ppermute x14, starting transfers between devices, with_halo(): lax.ppermute(tail, axis, [(i, (i + 1) % count) for i in range(count)])  9.67 us
    transpose x1, other arithmetic, read_back(): grid_field.reshape(EZ, 8, EA, 8, ER, 8).transpose(0, 2, 4, 1, 3, 5)  7.65 us
    slice x3, local copies, waits for them, and re-layouts, element_bound(): h_r = g_abs[4] * q_z + g_abs[5] * q_a + g_abs[2] * q_r  6.95 us
  transfers between devices with their start and end apart: 28, of which 16 were waited for; matrix products, arithmetic and copies ran while one was open for 13% of the time, Pallas kernels for 0%

commit v1 on v0

v1 whole, which is shorter than its diff:
```python
import functools

import jax
import jax.numpy as jnp
import numpy as np
from jax import lax
from jax.experimental import pallas as pl
from jax.experimental.pallas import tpu as pltpu
from jax.sharding import PartitionSpec as P

MESH = pl.DeviceIdType.MESH
interval_low = 0.03
interval_high = 1.0
FIELDS = 8
F32 = jnp.float32


def legendre_seven(point):
    before = 1.0
    current = point
    for degree in range(1, 7):
        after = ((2.0 * degree + 1.0) * point * current - degree * before) / (degree + 1.0)
        before = current
        current = after
    return current


def gll_derivative():
    points = 8
    inner_nodes = [
        -0.8717401485096066,
        -0.5917001814331423,
        -0.2092992179024789,
        0.2092992179024789,
        0.5917001814331423,
        0.8717401485096066,
    ]
    nodes = [-1.0] + inner_nodes + [1.0]
    values_at = [legendre_seven(node) for node in nodes]
    matrix = np.zeros((points, points))
    for source in range(points):
        for target in range(points):
            if source != target:
                matrix[source, target] = values_at[source] / (
                    values_at[target] * (nodes[source] - nodes[target])
                )
    matrix[0, 0] = -(points - 1) * points / 4.0
    matrix[points - 1, points - 1] = (points - 1) * points / 4.0
    return matrix


DERIV = gll_derivative()
ABS = np.abs(DERIV)
ROW_TOTAL = ABS.sum(axis=1)


def halves(matrix):
    even = (matrix[:4, :4] + matrix[:4, :3:-1]) / 2.0
    odd = (matrix[:4, :4] - matrix[:4, :3:-1]) / 2.0
    return even, odd


def combine(row, terms):
    total = terms[0] * float(row[0])
    for factor, term in zip(row[1:], terms[1:]):
        total = total + term * float(factor)
    return total


def along_eight(values, matrix, parity):
    even, odd = halves(matrix)
    sums = [values[m] + values[7 - m] for m in range(4)]
    differences = [values[m] - values[7 - m] for m in range(4)]
    result = [None] * 8
    for i in range(4):
        e = combine(even[i], sums)
        o = combine(odd[i], differences)
        result[i] = e + o
        result[7 - i] = (e - o) if parity > 0 else (o - e)
    return result


def lane_roll(value, shift):
    shape = value.shape
    flat = value.reshape(-1, shape[-1])
    return pltpu.roll(flat, shift, 1).reshape(shape)


def along_mirrored(value, matrix, sign):
    even, odd = halves(matrix)
    other = lane_roll(value, 64)
    plus, minus = value + other, value - other
    sums, differences = (plus, minus) if sign > 0 else (minus, plus)
    rows = []
    for j in range(4):
        rows.append(
            combine(even[j], [sums[m] for m in range(4)])
            + combine(odd[j], [differences[m] for m in range(4)])
        )
    return jnp.stack(rows)


def wide_factors(count):
    factors = []
    while count > 1:
        for factor in (4, 3, 2, 5, 7):
            if count % factor == 0:
                break
        else:
            factor = count
        factors.append(factor)
        count //= factor
    return factors


def body(
    n_wide,
    n_narrow,
    load_ref,
    geom_ref,
    order_ref,
    solution_ref,
    residual_ref,
    metric,
    work,
    radial_in,
    radial_out,
    fields,
    faces,
    res,
    binv,
    zed,
    dee,
    image,
    first,
    part,
    from_z,
    from_a,
    from_c,
    gathered,
    z_send,
    z_recv,
    a_send,
    a_recv,
    c_send,
    c_recv,
    g_send,
    g_recv,
):
    w = lax.axis_index("wide")
    n = lax.axis_index("narrow")
    up = lax.rem(w + 1, n_wide)
    down = lax.rem(w + n_wide - 1, n_wide)
    if n_narrow == 2:
        sides = [(lax.rem(n + 1, 2), 0)]
    else:
        sides = [(lax.rem(n + 1, n_narrow), 1), (lax.rem(n + n_narrow - 1, n_narrow), 2)]

    phases = []
    stride = 1
    for number, factor in enumerate(wide_factors(n_wide)):
        place = lax.rem(w // stride, factor)
        base = w - place * stride
        partners = []
        for dn in range(n_narrow if number == 0 else 1):
            for dw in range(factor):
                if dn == 0 and dw == 0:
                    continue
                there = base + lax.rem(place + dw, factor) * stride
                partners.append((there, lax.rem(n + dn, n_narrow)))
        phases.append(partners)
        stride *= factor

    barrier = pltpu.get_barrier_semaphore()
    greeted = [(up, n), (down, n)]
    for side, _ in sides:
        greeted += [(up, side), (down, side), (w, side)]
    for partners in phases:
        greeted += partners
    for device in greeted:
        pl.semaphore_signal(barrier, inc=1, device_id=device, device_id_type=MESH)

    lane = lax.broadcasted_iota(jnp.int32, (8, 128), 1)
    node = lax.broadcasted_iota(jnp.int32, (8, 128), 0)
    radial = lane % 16
    lane_row = lax.broadcasted_iota(jnp.int32, (1, 128), 1)
    mirror = jnp.where(lane_row < 64, 1.0, -1.0).astype(F32)
    radial_row = lane_row % 16

    order = order_ref[0].astype(jnp.int32)
    order_twice = jnp.concatenate([order, order + 64], axis=1)
    hot_t = (lax.broadcasted_iota(jnp.int32, (128, 128), 0) == order_twice).astype(F32)
    hot = jnp.transpose(hot_t)
    hot_both = (hot[:64] + hot[64:]).astype(jnp.bfloat16)
    top, bottom = hot[:64], hot[64:]
    zero = jnp.zeros_like(top)
    into_low = jnp.concatenate(
        [jnp.concatenate([top, zero], axis=1), jnp.concatenate([zero, top], axis=1)], axis=0
    ).astype(jnp.bfloat16)
    into_high = jnp.concatenate(
        [jnp.concatenate([bottom, zero], axis=1), jnp.concatenate([zero, bottom], axis=1)], axis=0
    ).astype(jnp.bfloat16)

    def place_pair(one, two):
        turned = jnp.transpose(jnp.concatenate([one, two], axis=0)).astype(jnp.bfloat16)
        split = turned.reshape(8, 8, 8, 128)
        low = split[:, :4].reshape(256, 128)
        high = jnp.stack([split[:, 7 - j] for j in range(4)], axis=1).reshape(256, 128)
        both = jnp.dot(low, into_low, preferred_element_type=F32)
        both = both + jnp.dot(high, into_high, preferred_element_type=F32)
        return both[:, :128], both[:, 128:]

    def rounded(value):
        return value.astype(jnp.bfloat16).astype(F32)

    load = load_ref[...]
    load_high = rounded(load)
    load_rest = load - load_high
    load_mid = rounded(load_rest)
    load_low = rounded(load_rest - load_mid)
    g = [geom_ref[q].astype(F32) for q in range(7)]
    for q in (0, 2, 4):
        metric[q], metric[q + 1] = place_pair(g[q], g[q + 1])
    metric[6], grid_high = place_pair(g[6], load_high)
    grid_mid, grid_low = place_pair(load_mid, load_low)
    fields[0] = grid_high + (grid_mid + grid_low)

    def slab(ref, i):
        return ref[pl.ds(32 * i, 32), :].reshape(4, 8, 128)

    def put(ref, i, value):
        ref[pl.ds(32 * i, 32), :] = value.reshape(32, 128)

    def radial_apply(matrix, parity):
        values = [radial_in[pl.ds(k, 32, stride=8), :] for k in range(8)]
        result = along_eight(values, matrix, parity)
        for k in range(8):
            radial_out[pl.ds(k, 32, stride=8), :] = result[k]

    q_r = jnp.full((8, 128), float(ROW_TOTAL[0]), F32)
    for k in range(1, 4):
        q_r = jnp.where((node == k) | (node == 7 - k), float(ROW_TOTAL[k]), q_r)
    h_z, part_a = [], []
    for i in range(8):
        a = [jnp.abs(slab(metric.at[q], i)) for q in range(6)]
        q_z = float(ROW_TOTAL[i])

        def by_cycle(value):
            return jnp.stack([value[j] * float(ROW_TOTAL[j]) for j in range(4)])

        h_z.append(a[0] * q_z + by_cycle(a[3]) + a[4] * q_r)
        part_a.append(along_mirrored(a[3] * q_z + by_cycle(a[1]) + a[5] * q_r, ABS.T, 1))
        put(radial_in, i, a[4] * q_z + by_cycle(a[5]) + a[2] * q_r)
    radial_apply(ABS.T, 1)
    part_z = along_eight(h_z, ABS.T, 1)
    for i in range(8):
        put(fields.at[1], i, part_z[i] + part_a[i] + slab(radial_out, i) + jnp.abs(slab(metric.at[6], i)))
    for q in (3, 5):
        metric[q] = metric[q] * mirror

    def element_apply(source, f):
        v = [slab(source, i) for i in range(8)]
        values = [source[pl.ds(k, 32, stride=8), :] for k in range(8)]
        result = along_eight(values, DERIV, -1)
        for k in range(8):
            radial_out[pl.ds(k, 32, stride=8), :] = result[k]
        grad_z = along_eight(v, DERIV, -1)
        flux_z, part_a = [], []
        for i in range(8):
            grad_a = along_mirrored(v[i], DERIV, 1)
            grad_r = slab(radial_out, i)
            g = [slab(metric.at[q], i) for q in range(6)]
            flux_z.append(g[0] * grad_z[i] + g[3] * grad_a + g[4] * grad_r)
            flux_a = g[3] * grad_z[i] + g[1] * grad_a + g[5] * grad_r
            put(radial_in, i, g[4] * grad_z[i] + g[5] * grad_a + g[2] * grad_r)
            part_a.append(along_mirrored(flux_a, DERIV.T, -1) + slab(metric.at[6], i) * v[i])
        radial_apply(DERIV.T, -1)
        part_z = along_eight(flux_z, DERIV.T, -1)
        energy = None
        for i in range(8):
            total = part_z[i] + part_a[i] + slab(radial_out, i)
            put(fields.at[f], i, total)
            term = jnp.sum(total * v[i], axis=0)
            energy = term if energy is None else energy + term
        return energy

    def assemble_own(f):
        ref = fields.at[f]
        inner = ref[pl.ds(0, 32, stride=8), :]
        outer = ref[pl.ds(7, 32, stride=8), :]
        ref[pl.ds(0, 32, stride=8), :] = inner + jnp.where(radial_row > 0, pltpu.roll(outer, 1, 1), 0.0)
        ref[pl.ds(7, 32, stride=8), :] = outer + jnp.where(radial_row < 15, pltpu.roll(inner, 127, 1), 0.0)
        for i in range(8):
            row = ref[pl.ds(32 * i, 8), :]
            below = pltpu.roll(row, 16, 1)
            above = pltpu.roll(row, 112, 1)
            for s, (_, kind) in enumerate(sides):
                message = jnp.zeros_like(row)
                if kind in (0, 1):
                    message = jnp.where(lane < 16, below, message)
                if kind in (0, 2):
                    message = jnp.where(lane >= 112, above, message)
                faces[f, s, pl.ds(8 * i, 8), :] = message
            inside = jnp.where(
                lane < 64, pltpu.roll(row, 80, 1), pltpu.roll(row, 48, 1)
            )
            ref[pl.ds(32 * i, 8), :] = row + jnp.where((lane >= 16) & (lane < 112), inside, 0.0)

    started = []

    def send(src, dst, send_sem, recv_sem, device):
        copy = pltpu.make_async_remote_copy(
            src_ref=src, dst_ref=dst, send_sem=send_sem, recv_sem=recv_sem, device_id=device, device_id_type=MESH
        )
        copy.start()
        started.append(copy)
        return copy

    def send_faces(f):
        copies = [
            send(fields.at[f, pl.ds(0, 32)], from_z.at[f, 1], z_send.at[f, 1], z_recv.at[f, 1], (down, n)),
            send(fields.at[f, pl.ds(224, 32)], from_z.at[f, 0], z_send.at[f, 0], z_recv.at[f, 0], (up, n)),
        ]
        for s, (side, _) in enumerate(sides):
            copies += [
                send(faces.at[f, s, pl.ds(0, 8)], from_c.at[f, s, 1], c_send.at[f, s, 1], c_recv.at[f, s, 1], (down, side)),
                send(faces.at[f, s, pl.ds(56, 8)], from_c.at[f, s, 0], c_send.at[f, s, 0], c_recv.at[f, s, 0], (up, side)),
            ]
        for s, (side, _) in enumerate(sides):
            copies.append(send(faces.at[f, s], from_a.at[f, s], a_send.at[f, s], a_recv.at[f, s], (w, side)))
        return copies

    def assembled(f, copies):
        for copy in copies:
            copy.wait_recv()
        result = []
        for i in range(8):
            value = slab(fields.at[f], i)
            if i == 0:
                value = value + from_z[f, 0].reshape(4, 8, 128)
            if i == 7:
                value = value + from_z[f, 1].reshape(4, 8, 128)
            row = value[0]
            for s in range(len(sides)):
                row = row + from_a[f, s, pl.ds(8 * i, 8), :]
                if i == 0:
                    row = row + from_c[f, s, 0]
                if i == 7:
                    row = row + from_c[f, s, 1]
            result.append(jnp.concatenate([row[None], value[1:]], axis=0))
        return result

    def weighted(one, two):
        total = None
        for i in range(8):
            product = one(i) * two(i)
            term = (product[1] + product[2]) + product[3] + product[0] * 0.5
            if i in (0, 7):
                term = term * 0.5
            total = term if total is None else total + term
        shared = ((node == 0) & (radial > 0)) | ((node == 7) & (radial < 15))
        return jnp.where(shared, total * 0.5, total)

    def stack_rows(terms):
        out = jnp.zeros((8, 128), F32)
        for q, term in enumerate(terms):
            out = jnp.where(node == q, jnp.sum(term, axis=0, keepdims=True), out)
        return out

    counts = [len(partners) for partners in phases]

    def sum_start(r, p, value):
        part[r, p] = value
        at = sum(counts[:p])
        return [
            send(part.at[r, p], gathered.at[r, at + q], g_send.at[r, at + q], g_recv.at[r, at + q], device)
            for q, device in enumerate(phases[p])
        ]

    def sum_end(r, p, copies):
        at = sum(counts[:p])
        total = part[r, p]
        for q, copy in enumerate(copies):
            copy.wait_recv()
            total = total + gathered[r, at + q]
        return total

    def sum_rest(r, p, copies):
        total = sum_end(r, p, copies)
        for later in range(p + 1, len(phases)):
            total = sum_end(r, later, sum_start(r, later, total))
        return jnp.sum(total, axis=1, keepdims=True)

    center = (interval_high + interval_low) / 2.0
    half_width = (interval_high - interval_low) / 2.0
    sigma = center / half_width
    rhos = [1.0 / sigma]
    for _ in range(2):
        rhos.append(1.0 / (2.0 * sigma - rhos[-1]))

    assemble_own(0)
    assemble_own(1)
    pl.semaphore_wait(barrier, len(greeted))
    copies = [send_faces(0), send_faces(1)]
    load_whole = assembled(0, copies[0])
    bound_whole = assembled(1, copies[1])
    for i in range(8):
        inverse = 1.0 / bound_whole[i]
        update = load_whole[i] * inverse * (1.0 / center)
        put(binv, i, inverse)
        put(res, i, load_whole[i])
        put(zed, i, update)
        put(dee, i, update)

    def smooth(f, source, step, between=None):
        element_apply(zed, f)
        assemble_own(f)
        copies = send_faces(f)
        after = between() if between is not None else None
        whole = assembled(f, copies)
        now, later = rhos[step], rhos[step + 1]
        for i in range(8):
            update = slab(dee, i) * (now * later) + slab(binv, i) * (slab(source, i) - whole[i]) * (
                2.0 * later / half_width
            )
            put(dee, i, update)
            put(zed, i, slab(zed, i) + update)
        return after

    smooth(2, res, 0)
    smooth(3, res, 1)
    first[...] = zed[...]
    norm = weighted(lambda i: slab(res, i), lambda i: slab(zed, i))
    energy = element_apply(zed, 4)
    assemble_own(4)
    copies = send_faces(4)
    sums = sum_start(0, 0, stack_rows([norm, energy]))
    whole = assembled(4, copies)
    for i in range(8):
        put(image, i, whole[i])
        update = whole[i] * slab(binv, i) * (1.0 / center)
        put(zed, i, update)
        put(dee, i, update)

    def next_phase():
        total = sum_end(0, 0, sums)
        return sum_start(0, 1, total)

    more = smooth(5, image, 0, next_phase)
    smooth(6, image, 1)
    total = sum_rest(0, 1, more)
    norm_0, energy_0 = total[0:1], total[1:2]
    alpha_0 = norm_0 / energy_0
    for i in range(8):
        put(res, i, slab(res, i) - alpha_0 * slab(image, i))
        put(zed, i, slab(first, i) - alpha_0 * slab(zed, i))
    norm = weighted(lambda i: slab(res, i), lambda i: slab(zed, i))
    cross = weighted(lambda i: slab(zed, i), lambda i: slab(image, i))
    energy = element_apply(zed, 7)
    assemble_own(7)
    copies = send_faces(7)
    sums = sum_start(1, 0, stack_rows([norm, cross, energy]))
    total = sum_rest(1, 0, sums)
    whole = assembled(7, copies)
    norm_1, cross_1, energy_1 = total[0:1], total[1:2], total[2:3]
    beta = norm_1 / norm_0
    alpha_1 = norm_1 / (energy_1 + 2.0 * beta * cross_1 + beta * beta * energy_0)

    def give(ref, value_of):
        rows = []
        for i in range(8):
            value = value_of(i)
            for j in range(8):
                keep = (lane < 64) if j < 4 else (lane >= 64)
                rows.append(jnp.where(keep, value[j if j < 4 else 7 - j], 0.0))
        full = jnp.stack(rows).reshape(512, 128)
        high = full.astype(jnp.bfloat16)
        low = (full - high.astype(F32)).astype(jnp.bfloat16)
        dims = (((1,), (1,)), ((), ()))
        ref[...] = lax.dot_general(hot_both, high, dims, preferred_element_type=F32) + lax.dot_general(
            hot_both, low, dims, preferred_element_type=F32
        )

    give(
        solution_ref,
        lambda i: alpha_0 * slab(first, i) + alpha_1 * (slab(zed, i) + beta * slab(first, i)),
    )
    give(residual_ref, lambda i: slab(res, i) - alpha_1 * (whole[i] + beta * slab(image, i)))
    for copy in started:
        copy.wait_send()


def solution(mesh):
    n_wide, n_narrow = mesh.shape["wide"], mesh.shape["narrow"]
    sides = 1 if n_narrow == 2 else 2
    factors = wide_factors(n_wide)
    partners = n_narrow * factors[0] - 1 + sum(factor - 1 for factor in factors[1:])
    vmem = pltpu.VMEM
    block = vmem((256, 128), F32)
    dma = pltpu.SemaphoreType.DMA

    def local(load, geom, element_order):
        whole = pl.BlockSpec(memory_space=pltpu.VMEM)
        shape = jax.ShapeDtypeStruct(load.shape, F32)
        return pl.pallas_call(
            functools.partial(body, n_wide, n_narrow),
            out_shape=(shape, shape),
            in_specs=[whole] * 3,
            out_specs=(whole, whole),
            scratch_shapes=[
                vmem((7, 256, 128), F32),
                block,
                block,
                block,
                vmem((FIELDS, 256, 128), F32),
                vmem((FIELDS, sides, 64, 128), F32),
                block,
                block,
                block,
                block,
                block,
                block,
                vmem((2, len(factors), 8, 128), F32),
                vmem((FIELDS, 2, 32, 128), F32),
                vmem((FIELDS, sides, 64, 128), F32),
                vmem((FIELDS, sides, 2, 8, 128), F32),
                vmem((2, partners, 8, 128), F32),
                dma((FIELDS, 2)),
                dma((FIELDS, 2)),
                dma((FIELDS, sides)),
                dma((FIELDS, sides)),
                dma((FIELDS, sides, 2)),
                dma((FIELDS, sides, 2)),
                dma((2, partners)),
                dma((2, partners)),
            ],
            compiler_params=pltpu.CompilerParams(
                collective_id=0, has_side_effects=True, vmem_limit_bytes=32 * 1024 * 1024
            ),
        )(load, geom, element_order)

    return jax.shard_map(
        local,
        mesh=mesh,
        in_specs=(
            P(("wide", "narrow"), None),
            P(None, ("wide", "narrow"), None),
            P("wide", "narrow", None),
        ),
        out_specs=(P(("wide", "narrow"), None), P(("wide", "narrow"), None)),
        check_vma=False,
    )
```

time: 320 us -> 50 us (0.16)
  blocking collectives: 121 us -> 0 us
  local copies, waits for them, and re-layouts: 87.8 us -> 3.88 us
  Pallas kernels: 0 us -> 45.3 us
  starting transfers between devices: 45.3 us -> 0 us
  other arithmetic: 29.5 us -> 0 us
  waiting for transfers between devices: 13.6 us -> 0 us
  matrix products: 12.8 us -> 0 us
  between operations: 6.45 us -> 0.65 us
    psum x3 -> x0, blocking collectives: 121 us -> none  [the longest x2 80.8 us: local(): precond_norm = lax.psum(inner(grid_residual, result), ('wide', 'narrow'))]
    pallas_call x0 -> x1, Pallas kernels: none -> 45.3 us  [local(): pl.pallas_call(functools.partial(body, n_wide, n_narrow), out_shape=(shap...]
    ppermute x28 -> x0, starting transfers between devices: 45.3 us -> none  [the longest x14 35.6 us: with_halo(): lax.ppermute(head, axis, [((i + 1) % count, i) for i in range(count)])]
    convert_element_type x14 -> x0, local copies, waits for them, and re-layouts: 20.2 us -> none  [the longest x2 2.91 us: element_apply(): g_za = metric[3].astype(jnp.float32)]
    slice x17 -> x0, local copies, waits for them, and re-layouts: 20.2 us -> none  [the longest x3 6.95 us: element_bound(): h_r = g_abs[4] * q_z + g_abs[5] * q_a + g_abs[2] * q_r]
    squeeze x11 -> x0, local copies, waits for them, and re-layouts: 19.2 us -> none  [the longest x4 9.94 us: operator(): assemble(element_apply(field, metric, derivative, radial_matrix)[None])[0]]
    ppermute x28 -> x0, waiting for transfers between devices: 13.6 us -> none  [the longest x14 12.8 us: with_halo(): lax.ppermute(tail, axis, [(i, (i + 1) % count) for i in range(count)])]
    dot_general x39 -> x0, matrix products: 12.8 us -> none  [the longest x13 4.78 us: radial_apply(): jnp.dot(flat, radial_matrix, precision=lax.Precision.HIGHEST, preferred_e...]
  transfers between devices with their start and end apart: 28 -> 0, of which waited for: 16 -> 0; matrix products, arithmetic and copies ran while one was open for 13% -> 0% of each run, Pallas kernels for 0% -> 0%
where the time goes in v1:
time: 50 us; the launch traced here: 49.9 us
  Pallas kernels  45.3 us (91%)
  local copies, waits for them, and re-layouts  3.88 us (8%)
  between operations  0.65 us (1%)
    pallas_call x1, Pallas kernels, local(): pl.pallas_call(functools.partial(body, n_wide, n_narrow), out_shape=(shap...  45.3 us
    unnamed x8, local copies, waits for them, and re-layouts  3.88 us

profile of v1, /device:TPU:0, one launch (start us, length us, event | category | flops | bytes accessed | tf_op | source)
XLA Modules:
  0.0 49.9 jit_solution(10902613695996526335)
XLA Ops:
  0.6 0.0 copy-start
  0.6 1.0 %copy-done = bf16[7,64,512]{2,1,0:T(8,128)(2,1)S(1)} copy-done((bf16[7,64,512]{2,1,0:T(8,128)(2,1)S(1)}, bf16[7,64,512]{2,1,0:T(8,128)(2,1)}, u32[]{:S(2)}) %copy-start) | copy-done | bytes 458776
  1.6 0.0 copy-start.1
  1.7 0.9 %copy-done.1 = f32[64,512]{1,0:T(8,128)S(1)} copy-done((f32[64,512]{1,0:T(8,128)S(1)}, f32[64,512]{1,0:T(8,128)}, u32[]{:S(2)}) %copy-start.1) | copy-done | bytes 131096
  2.6 0.0 copy-start.2
  2.6 0.7 %copy-done.2 = s32[1,1,64]{2,1,0:T(1,128)S(1)} copy-done((s32[1,1,64]{2,1,0:T(1,128)S(1)}, s32[1,1,64]{2,1,0:T(1,128)}, u32[]{:S(2)}) %copy-start.2) | copy-done | bytes 280
  3.2 45.3 %shard_map.50 = (f32[64,512]{1,0:T(8,128)S(1)}, f32[64,512]{1,0:T(8,128)S(1)}) custom-call(f32[64,512]{1,0:T(8,128)S(1)} %copy-done.1, bf16[7,64,512]{2,1,0:T(8,128)(2,1)S(1)} %copy-done, s32[1,1,64]{2,1,0:T(1,128)S(1)} %copy-done.2), custom_call_target="tpu_custom_call" | custom-call | tf_op jit(solution)/shard_map/pallas_call | solution.py:505
  48.5 0.7 %copy.7 = f32[64,512]{1,0:T(8,128)} copy(f32[64,512]{1,0:T(8,128)S(1)} %get-tuple-element.4) | data formatting | bytes 262144
  49.2 0.7 %copy.8 = f32[64,512]{1,0:T(8,128)} copy(f32[64,512]{1,0:T(8,128)S(1)} %get-tuple-element.5) | data formatting | bytes 262144
Async XLA Ops:
  0.6 1.0 %copy-start = (bf16[7,64,512]{2,1,0:T(8,128)(2,1)S(1)}, bf16[7,64,512]{2,1,0:T(8,128)(2,1)}, u32[]{:S(2)}) copy-start(bf16[7,64,512]{2,1,0:T(8,128)(2,1)} %geom_ref.1) | copy-start | bytes 1376260
  1.6 0.9 %copy-start.1 = (f32[64,512]{1,0:T(8,128)S(1)}, f32[64,512]{1,0:T(8,128)}, u32[]{:S(2)}) copy-start(f32[64,512]{1,0:T(8,128)} %load_ref.1) | copy-start | bytes 393220
  2.6 0.7 %copy-start.2 = (s32[1,1,64]{2,1,0:T(1,128)S(1)}, s32[1,1,64]{2,1,0:T(1,128)}, u32[]{:S(2)}) copy-start(s32[1,1,64]{2,1,0:T(1,128)} %order_ref.1) | copy-start | bytes 772

commit v2 on v1

--- a/solution.py
+++ b/solution.py
@@ -13,6 +13,12 @@
 interval_high = 1.0
 FIELDS = 8
 F32 = jnp.float32
+
+
+ORDER = [0, 7, 1, 6, 2, 5, 3, 4]
+POS = [ORDER.index(i) for i in range(8)]
+FACE = [0, 7]
+INNER = [1, 6, 2, 5, 3, 4]
 
 
 def legendre_seven(point):
@@ -116,15 +122,21 @@
 def body(
     n_wide,
     n_narrow,
+    load_hbm,
+    geom_hbm,
+    order_hbm,
+    solution_ref,
+    residual_ref,
     load_ref,
     geom_ref,
     order_ref,
-    solution_ref,
-    residual_ref,
     metric,
-    work,
     radial_in,
     radial_out,
+    part_fz,
+    part_fa,
+    part_fr,
+    grad_z,
     fields,
     faces,
     res,
@@ -133,6 +145,7 @@
     dee,
     image,
     first,
+    read,
     part,
     from_z,
     from_a,
@@ -146,7 +159,15 @@
     c_recv,
     g_send,
     g_recv,
+    in_sem,
 ):
+    fetches = [
+        pltpu.make_async_copy(order_hbm, order_ref, in_sem.at[0]),
+        pltpu.make_async_copy(load_hbm, load_ref, in_sem.at[1]),
+        pltpu.make_async_copy(geom_hbm, geom_ref, in_sem.at[2]),
+    ]
+    for fetch in fetches:
+        fetch.start()
     w = lax.axis_index("wide")
     n = lax.axis_index("narrow")
     up = lax.rem(w + 1, n_wide)
@@ -187,6 +208,8 @@
     mirror = jnp.where(lane_row < 64, 1.0, -1.0).astype(F32)
     radial_row = lane_row % 16
 
+    for fetch in fetches:
+        fetch.wait()
     order = order_ref[0].astype(jnp.int32)
     order_twice = jnp.concatenate([order, order + 64], axis=1)
     hot_t = (lax.broadcasted_iota(jnp.int32, (128, 128), 0) == order_twice).astype(F32)
@@ -204,8 +227,8 @@
     def place_pair(one, two):
         turned = jnp.transpose(jnp.concatenate([one, two], axis=0)).astype(jnp.bfloat16)
         split = turned.reshape(8, 8, 8, 128)
-        low = split[:, :4].reshape(256, 128)
-        high = jnp.stack([split[:, 7 - j] for j in range(4)], axis=1).reshape(256, 128)
+        low = jnp.stack([split[i, j] for i in ORDER for j in range(4)]).reshape(256, 128)
+        high = jnp.stack([split[i, 7 - j] for i in ORDER for j in range(4)]).reshape(256, 128)
         both = jnp.dot(low, into_low, preferred_element_type=F32)
         both = both + jnp.dot(high, into_high, preferred_element_type=F32)
         return both[:, :128], both[:, 128:]
@@ -226,16 +249,16 @@
     fields[0] = grid_high + (grid_mid + grid_low)
 
     def slab(ref, i):
-        return ref[pl.ds(32 * i, 32), :].reshape(4, 8, 128)
+        return ref[pl.ds(32 * POS[i], 32), :].reshape(4, 8, 128)
 
     def put(ref, i, value):
-        ref[pl.ds(32 * i, 32), :] = value.reshape(32, 128)
-
-    def radial_apply(matrix, parity):
-        values = [radial_in[pl.ds(k, 32, stride=8), :] for k in range(8)]
+        ref[pl.ds(32 * POS[i], 32), :] = value.reshape(32, 128)
+
+    def radial_apply(source, matrix, parity, start=0, count=32):
+        values = [source[pl.ds(8 * start + k, count, stride=8), :] for k in range(8)]
         result = along_eight(values, matrix, parity)
         for k in range(8):
-            radial_out[pl.ds(k, 32, stride=8), :] = result[k]
+            radial_out[pl.ds(8 * start + k, count, stride=8), :] = result[k]
 
     q_r = jnp.full((8, 128), float(ROW_TOTAL[0]), F32)
     for k in range(1, 4):
@@ -251,47 +274,105 @@
         h_z.append(a[0] * q_z + by_cycle(a[3]) + a[4] * q_r)
         part_a.append(along_mirrored(a[3] * q_z + by_cycle(a[1]) + a[5] * q_r, ABS.T, 1))
         put(radial_in, i, a[4] * q_z + by_cycle(a[5]) + a[2] * q_r)
-    radial_apply(ABS.T, 1)
+    radial_apply(radial_in, ABS.T, 1)
     part_z = along_eight(h_z, ABS.T, 1)
     for i in range(8):
         put(fields.at[1], i, part_z[i] + part_a[i] + slab(radial_out, i) + jnp.abs(slab(metric.at[6], i)))
     for q in (3, 5):
         metric[q] = metric[q] * mirror
 
-    def element_apply(source, f):
-        v = [slab(source, i) for i in range(8)]
-        values = [source[pl.ds(k, 32, stride=8), :] for k in range(8)]
-        result = along_eight(values, DERIV, -1)
-        for k in range(8):
-            radial_out[pl.ds(k, 32, stride=8), :] = result[k]
-        grad_z = along_eight(v, DERIV, -1)
-        flux_z, part_a = [], []
-        for i in range(8):
-            grad_a = along_mirrored(v[i], DERIV, 1)
+    even, odd = halves(DERIV)
+    even_t, odd_t = halves(DERIV.T)
+
+    def forward_inner():
+        radial_apply(zed, DERIV, -1, 8, 24)
+        for i in INNER:
+            grad_a = along_mirrored(slab(zed, i), DERIV, 1)
             grad_r = slab(radial_out, i)
-            g = [slab(metric.at[q], i) for q in range(6)]
-            flux_z.append(g[0] * grad_z[i] + g[3] * grad_a + g[4] * grad_r)
-            flux_a = g[3] * grad_z[i] + g[1] * grad_a + g[5] * grad_r
-            put(radial_in, i, g[4] * grad_z[i] + g[5] * grad_a + g[2] * grad_r)
-            part_a.append(along_mirrored(flux_a, DERIV.T, -1) + slab(metric.at[6], i) * v[i])
-        radial_apply(DERIV.T, -1)
-        part_z = along_eight(flux_z, DERIV.T, -1)
-        energy = None
-        for i in range(8):
-            total = part_z[i] + part_a[i] + slab(radial_out, i)
+            put(part_fz, i, slab(metric.at[3], i) * grad_a + slab(metric.at[4], i) * grad_r)
+            put(part_fa, i, slab(metric.at[1], i) * grad_a + slab(metric.at[5], i) * grad_r)
+            put(part_fr, i, slab(metric.at[5], i) * grad_a + slab(metric.at[2], i) * grad_r)
+        for j in range(4):
+            v = [tile(zed, i, j) for i in range(1, 7)]
+            sums = [v[m] + v[5 - m] for m in range(3)]
+            differences = [v[m] - v[5 - m] for m in range(3)]
+            for i in range(4):
+                e, o = combine(even[i][1:], sums), combine(odd[i][1:], differences)
+                put_tile(grad_z, i, j, e + o)
+                put_tile(grad_z, 7 - i, j, o - e)
+
+    def tile(ref, i, j):
+        return ref[pl.ds(32 * POS[i] + 8 * j, 8), :]
+
+    def put_tile(ref, i, j, value):
+        ref[pl.ds(32 * POS[i] + 8 * j, 8), :] = value
+
+    def forward_face(f):
+        radial_apply(zed, DERIV, -1, 0, 8)
+        grad_a = {i: along_mirrored(slab(zed, i), DERIV, 1) for i in FACE}
+        energy = jnp.zeros((8, 128), F32)
+        flux_a = {i: [] for i in FACE}
+        pieces = {i: [] for i in FACE}
+        for j in range(4):
+            v0, v7 = tile(zed, 0, j), tile(zed, 7, j)
+            plus, minus = v0 + v7, v0 - v7
+            flux_z = [None] * 8
+            for i in range(4):
+                e, o = plus * float(even[i][0]), minus * float(odd[i][0])
+                for node_i, extra in ((i, e + o), (7 - i, o - e)):
+                    slope = tile(grad_z, node_i, j) + extra
+                    put_tile(grad_z, node_i, j, slope)
+                    if node_i in FACE:
+                        g = [tile(metric.at[q], node_i, j) for q in range(6)]
+                        slope_a = grad_a[node_i][j]
+                        slope_r = tile(radial_out, node_i, j)
+                        flux = g[0] * slope + g[3] * slope_a + g[4] * slope_r
+                        flux_a[node_i].append(g[3] * slope + g[1] * slope_a + g[5] * slope_r)
+                        put_tile(radial_in, node_i, j, g[4] * slope + g[5] * slope_a + g[2] * slope_r)
+                    else:
+                        flux = tile(part_fz, node_i, j) + tile(metric.at[0], node_i, j) * slope
+                    put_tile(part_fz, node_i, j, flux)
+                    flux_z[node_i] = flux
+            e = combine(even_t[0], [flux_z[m] + flux_z[7 - m] for m in range(4)])
+            o = combine(odd_t[0], [flux_z[m] - flux_z[7 - m] for m in range(4)])
+            pieces[0].append(e + o + tile(metric.at[6], 0, j) * v0)
+            pieces[7].append(o - e + tile(metric.at[6], 7, j) * v7)
+        radial_apply(radial_in, DERIV.T, -1, 0, 8)
+        for i in FACE:
+            total = jnp.stack(pieces[i]) + along_mirrored(jnp.stack(flux_a[i]), DERIV.T, -1) + slab(radial_out, i)
             put(fields.at[f], i, total)
-            term = jnp.sum(total * v[i], axis=0)
-            energy = term if energy is None else energy + term
+            energy = energy + jnp.sum(total * slab(zed, i), axis=0)
         return energy
 
-    def assemble_own(f):
+    def forward_rest(f):
+        energy = jnp.zeros((8, 128), F32)
+        for i in INNER:
+            slope = slab(grad_z, i)
+            flux_a = slab(part_fa, i) + slab(metric.at[3], i) * slope
+            put(radial_in, i, slab(part_fr, i) + slab(metric.at[4], i) * slope)
+            put(part_fa, i, along_mirrored(flux_a, DERIV.T, -1) + slab(metric.at[6], i) * slab(zed, i))
+        radial_apply(radial_in, DERIV.T, -1, 8, 24)
+        for j in range(4):
+            flux_z = [tile(part_fz, i, j) for i in range(8)]
+            sums = [flux_z[m] + flux_z[7 - m] for m in range(4)]
+            differences = [flux_z[m] - flux_z[7 - m] for m in range(4)]
+            for i in range(1, 4):
+                e, o = combine(even_t[i], sums), combine(odd_t[i], differences)
+                for node_i, piece in ((i, e + o), (7 - i, o - e)):
+                    total = piece + tile(part_fa, node_i, j) + tile(radial_out, node_i, j)
+                    put_tile(fields.at[f], node_i, j, total)
+                    energy = energy + total * tile(zed, node_i, j)
+        return energy
+
+    def assemble_own(f, start, count):
         ref = fields.at[f]
-        inner = ref[pl.ds(0, 32, stride=8), :]
-        outer = ref[pl.ds(7, 32, stride=8), :]
-        ref[pl.ds(0, 32, stride=8), :] = inner + jnp.where(radial_row > 0, pltpu.roll(outer, 1, 1), 0.0)
-        ref[pl.ds(7, 32, stride=8), :] = outer + jnp.where(radial_row < 15, pltpu.roll(inner, 127, 1), 0.0)
-        for i in range(8):
-            row = ref[pl.ds(32 * i, 8), :]
+        low = pl.ds(8 * start, count, stride=8)
+        high = pl.ds(8 * start + 7, count, stride=8)
+        inner, outer = ref[low, :], ref[high, :]
+        ref[low, :] = inner + jnp.where(radial_row > 0, pltpu.roll(outer, 1, 1), 0.0)
+        ref[high, :] = outer + jnp.where(radial_row < 15, pltpu.roll(inner, 127, 1), 0.0)
+        for at in range(start // 4, (start + count) // 4):
+            row = ref[pl.ds(32 * at, 8), :]
             below = pltpu.roll(row, 16, 1)
             above = pltpu.roll(row, 112, 1)
             for s, (_, kind) in enumerate(sides):
@@ -300,11 +381,9 @@
                     message = jnp.where(lane < 16, below, message)
                 if kind in (0, 2):
                     message = jnp.where(lane >= 112, above, message)
-                faces[f, s, pl.ds(8 * i, 8), :] = message
-            inside = jnp.where(
-                lane < 64, pltpu.roll(row, 80, 1), pltpu.roll(row, 48, 1)
-            )
-            ref[pl.ds(32 * i, 8), :] = row + jnp.where((lane >= 16) & (lane < 112), inside, 0.0)
+                faces[f, s, pl.ds(8 * at, 8), :] = message
+            inside = jnp.where(lane < 64, pltpu.roll(row, 80, 1), pltpu.roll(row, 48, 1))
+            ref[pl.ds(32 * at, 8), :] = row + jnp.where((lane >= 16) & (lane < 112), inside, 0.0)
 
     started = []
 
@@ -316,39 +395,40 @@
         started.append(copy)
         return copy
 
-    def send_faces(f):
+    def send_pipe(f):
         copies = [
             send(fields.at[f, pl.ds(0, 32)], from_z.at[f, 1], z_send.at[f, 1], z_recv.at[f, 1], (down, n)),
-            send(fields.at[f, pl.ds(224, 32)], from_z.at[f, 0], z_send.at[f, 0], z_recv.at[f, 0], (up, n)),
+            send(fields.at[f, pl.ds(32, 32)], from_z.at[f, 0], z_send.at[f, 0], z_recv.at[f, 0], (up, n)),
         ]
         for s, (side, _) in enumerate(sides):
             copies += [
                 send(faces.at[f, s, pl.ds(0, 8)], from_c.at[f, s, 1], c_send.at[f, s, 1], c_recv.at[f, s, 1], (down, side)),
-                send(faces.at[f, s, pl.ds(56, 8)], from_c.at[f, s, 0], c_send.at[f, s, 0], c_recv.at[f, s, 0], (up, side)),
+                send(faces.at[f, s, pl.ds(8, 8)], from_c.at[f, s, 0], c_send.at[f, s, 0], c_recv.at[f, s, 0], (up, side)),
             ]
-        for s, (side, _) in enumerate(sides):
-            copies.append(send(faces.at[f, s], from_a.at[f, s], a_send.at[f, s], a_recv.at[f, s], (w, side)))
         return copies
 
-    def assembled(f, copies):
+    def send_cycle(f):
+        return [
+            send(faces.at[f, s], from_a.at[f, s], a_send.at[f, s], a_recv.at[f, s], (w, side))
+            for s, (side, _) in enumerate(sides)
+        ]
+
+    def whole_plane(f, i):
+        value = slab(fields.at[f], i)
+        row = value[0]
+        for s in range(len(sides)):
+            row = row + from_a[f, s, pl.ds(8 * POS[i], 8), :]
+        if i in FACE:
+            come = from_z[f, POS[i]].reshape(4, 8, 128)
+            row = row + come[0]
+            for s in range(len(sides)):
+                row = row + from_c[f, s, POS[i]]
+            return jnp.concatenate([row[None], value[1:] + come[1:]], axis=0)
+        return jnp.concatenate([row[None], value[1:]], axis=0)
+
+    def wait_all(copies):
         for copy in copies:
             copy.wait_recv()
-        result = []
-        for i in range(8):
-            value = slab(fields.at[f], i)
-            if i == 0:
-                value = value + from_z[f, 0].reshape(4, 8, 128)
-            if i == 7:
-                value = value + from_z[f, 1].reshape(4, 8, 128)
-            row = value[0]
-            for s in range(len(sides)):
-                row = row + from_a[f, s, pl.ds(8 * i, 8), :]
-                if i == 0:
-                    row = row + from_c[f, s, 0]
-                if i == 7:
-                    row = row + from_c[f, s, 1]
-            result.append(jnp.concatenate([row[None], value[1:]], axis=0))
-        return result
 
     def weighted(one, two):
         total = None
@@ -398,94 +478,134 @@
     for _ in range(2):
         rhos.append(1.0 / (2.0 * sigma - rhos[-1]))
 
-    assemble_own(0)
-    assemble_own(1)
+    assemble_own(0, 0, 32)
+    assemble_own(1, 0, 32)
     pl.semaphore_wait(barrier, len(greeted))
-    copies = [send_faces(0), send_faces(1)]
-    load_whole = assembled(0, copies[0])
-    bound_whole = assembled(1, copies[1])
-    for i in range(8):
-        inverse = 1.0 / bound_whole[i]
-        update = load_whole[i] * inverse * (1.0 / center)
+    pipe = send_pipe(1) + send_pipe(0)
+    cycle = send_cycle(1) + send_cycle(0)
+
+    def begin(i):
+        inverse = 1.0 / whole_plane(1, i)
+        load_plane = whole_plane(0, i)
+        update = load_plane * inverse * (1.0 / center)
         put(binv, i, inverse)
-        put(res, i, load_whole[i])
+        put(res, i, load_plane)
         put(zed, i, update)
         put(dee, i, update)
 
-    def smooth(f, source, step, between=None):
-        element_apply(zed, f)
-        assemble_own(f)
-        copies = send_faces(f)
-        after = between() if between is not None else None
-        whole = assembled(f, copies)
+    wait_all(cycle)
+    for i in INNER:
+        begin(i)
+    forward_inner()
+    wait_all(pipe)
+    for i in FACE:
+        begin(i)
+
+    def apply_then(f, update, between=None, last=None):
+        energy = forward_face(f)
+        assemble_own(f, 0, 8)
+        pipe = send_pipe(f)
+        energy = energy + forward_rest(f)
+        assemble_own(f, 8, 24)
+        cycle = send_cycle(f)
+        after = between(energy) if between is not None else None
+        wait_all(cycle)
+        for i in INNER:
+            update(i, whole_plane(f, i))
+        forward_inner()
+        wait_all(pipe)
+        for i in FACE:
+            update(i, whole_plane(f, i))
+        return after
+
+    def smoothed(source, step, i, plane):
         now, later = rhos[step], rhos[step + 1]
-        for i in range(8):
-            update = slab(dee, i) * (now * later) + slab(binv, i) * (slab(source, i) - whole[i]) * (
-                2.0 * later / half_width
-            )
-            put(dee, i, update)
-            put(zed, i, slab(zed, i) + update)
-        return after
-
-    smooth(2, res, 0)
-    smooth(3, res, 1)
-    first[...] = zed[...]
-    norm = weighted(lambda i: slab(res, i), lambda i: slab(zed, i))
-    energy = element_apply(zed, 4)
-    assemble_own(4)
-    copies = send_faces(4)
-    sums = sum_start(0, 0, stack_rows([norm, energy]))
-    whole = assembled(4, copies)
-    for i in range(8):
-        put(image, i, whole[i])
-        update = whole[i] * slab(binv, i) * (1.0 / center)
+        return slab(dee, i) * (now * later) + slab(binv, i) * (slab(source, i) - plane) * (2.0 * later / half_width)
+
+    def smooth(source, step):
+        def update(i, plane):
+            change = smoothed(source, step, i, plane)
+            put(dee, i, change)
+            put(zed, i, slab(zed, i) + change)
+
+        return update
+
+    apply_then(2, smooth(res, 0))
+    apply_then(3, smooth(res, 1))
+
+    def start_norm(energy):
+        norm = weighted(lambda i: slab(res, i), lambda i: slab(zed, i))
+        return sum_start(0, 0, stack_rows([norm, energy]))
+
+    def restart(i, plane):
+        put(image, i, plane)
+        put(first, i, slab(zed, i))
+        update = plane * slab(binv, i) * (1.0 / center)
         put(zed, i, update)
         put(dee, i, update)
 
-    def next_phase():
-        total = sum_end(0, 0, sums)
-        return sum_start(0, 1, total)
-
-    more = smooth(5, image, 0, next_phase)
-    smooth(6, image, 1)
-    total = sum_rest(0, 1, more)
-    norm_0, energy_0 = total[0:1], total[1:2]
-    alpha_0 = norm_0 / energy_0
-    for i in range(8):
-        put(res, i, slab(res, i) - alpha_0 * slab(image, i))
-        put(zed, i, slab(first, i) - alpha_0 * slab(zed, i))
-    norm = weighted(lambda i: slab(res, i), lambda i: slab(zed, i))
-    cross = weighted(lambda i: slab(zed, i), lambda i: slab(image, i))
-    energy = element_apply(zed, 7)
-    assemble_own(7)
-    copies = send_faces(7)
-    sums = sum_start(1, 0, stack_rows([norm, cross, energy]))
-    total = sum_rest(1, 0, sums)
-    whole = assembled(7, copies)
-    norm_1, cross_1, energy_1 = total[0:1], total[1:2], total[2:3]
-    beta = norm_1 / norm_0
-    alpha_1 = norm_1 / (energy_1 + 2.0 * beta * cross_1 + beta * beta * energy_0)
-
-    def give(ref, value_of):
+    sums = apply_then(4, restart, start_norm)
+    more = apply_then(5, smooth(image, 0), lambda energy: sum_start(0, 1, sum_end(0, 0, sums)))
+    scalars = {}
+
+    def finish_norm(energy):
+        total = sum_rest(0, 1, more)
+        scalars["norm"], scalars["energy"] = total[0:1], total[1:2]
+        scalars["alpha"] = total[0:1] / total[1:2]
+
+    def step_on(i, plane):
+        end = slab(zed, i) + smoothed(image, 1, i, plane)
+        put(res, i, slab(res, i) - scalars["alpha"] * slab(image, i))
+        put(zed, i, slab(first, i) - scalars["alpha"] * end)
+
+    apply_then(6, step_on, finish_norm)
+    norm_0, energy_0, alpha_0 = scalars["norm"], scalars["energy"], scalars["alpha"]
+
+    def read_back(value_of, planes):
         rows = []
-        for i in range(8):
+        for i in planes:
             value = value_of(i)
             for j in range(8):
                 keep = (lane < 64) if j < 4 else (lane >= 64)
                 rows.append(jnp.where(keep, value[j if j < 4 else 7 - j], 0.0))
-        full = jnp.stack(rows).reshape(512, 128)
+        full = jnp.stack(rows).reshape(64 * len(planes), 128)
         high = full.astype(jnp.bfloat16)
         low = (full - high.astype(F32)).astype(jnp.bfloat16)
         dims = (((1,), (1,)), ((), ()))
-        ref[...] = lax.dot_general(hot_both, high, dims, preferred_element_type=F32) + lax.dot_general(
+        return lax.dot_general(hot_both, high, dims, preferred_element_type=F32) + lax.dot_general(
             hot_both, low, dims, preferred_element_type=F32
         )
 
-    give(
-        solution_ref,
-        lambda i: alpha_0 * slab(first, i) + alpha_1 * (slab(zed, i) + beta * slab(first, i)),
-    )
-    give(residual_ref, lambda i: slab(res, i) - alpha_1 * (whole[i] + beta * slab(image, i)))
+    energy = forward_face(7)
+    assemble_own(7, 0, 8)
+    pipe = send_pipe(7)
+    energy = energy + forward_rest(7)
+    norm = weighted(lambda i: slab(res, i), lambda i: slab(zed, i))
+    cross = weighted(lambda i: slab(zed, i), lambda i: slab(image, i))
+    sums = sum_start(1, 0, stack_rows([norm, cross, energy]))
+    assemble_own(7, 8, 24)
+    cycle = send_cycle(7)
+    for q, ref in enumerate((first, zed)):
+        read[q] = read_back(lambda i: slab(ref, i), range(8))
+    totals = sum_end(1, 0, sums)
+    for later in range(1, len(phases) - 1):
+        totals = sum_end(1, later, sum_start(1, later, totals))
+    sums = sum_start(1, len(phases) - 1, totals)
+    for q, ref in enumerate((res, image)):
+        read[2 + q] = read_back(lambda i: slab(ref, i), range(8))
+    wait_all(cycle)
+    middle = read_back(lambda i: whole_plane(7, i), range(2, 6))
+    total = jnp.sum(sum_end(1, len(phases) - 1, sums), axis=1, keepdims=True)
+    norm_1, cross_1, energy_1 = total[0:1], total[1:2], total[2:3]
+    beta = norm_1 / norm_0
+    alpha_1 = norm_1 / (energy_1 + 2.0 * beta * cross_1 + beta * beta * energy_0)
+    solution_ref[...] = (alpha_0 + alpha_1 * beta) * read[0] + alpha_1 * read[1]
+    residual = read[2] - (alpha_1 * beta) * read[3]
+    residual_ref[:, 128:384] = residual[:, 128:384] - alpha_1 * middle
+    wait_all(pipe)
+    ends = read_back(lambda i: whole_plane(7, i), (0, 1, 6, 7))
+    residual_ref[:, 0:128] = residual[:, 0:128] - alpha_1 * ends[:, 0:128]
+    residual_ref[:, 384:512] = residual[:, 384:512] - alpha_1 * ends[:, 128:256]
     for copy in started:
         copy.wait_send()
 
@@ -505,10 +625,16 @@
         return pl.pallas_call(
             functools.partial(body, n_wide, n_narrow),
             out_shape=(shape, shape),
-            in_specs=[whole] * 3,
+            in_specs=[pl.BlockSpec(memory_space=pltpu.HBM)] * 3,
             out_specs=(whole, whole),
             scratch_shapes=[
+                vmem(load.shape, F32),
+                vmem(geom.shape, geom.dtype),
+                vmem(element_order.shape, jnp.int32),
                 vmem((7, 256, 128), F32),
+                block,
+                block,
+                block,
                 block,
                 block,
                 block,
@@ -520,6 +646,7 @@
                 block,
                 block,
                 block,
+                vmem((4, 64, 512), F32),
                 vmem((2, len(factors), 8, 128), F32),
                 vmem((FIELDS, 2, 32, 128), F32),
                 vmem((FIELDS, sides, 64, 128), F32),
@@ -533,6 +660,7 @@
                 dma((FIELDS, sides, 2)),
                 dma((2, partners)),
                 dma((2, partners)),
+                dma((3,)),
             ],
             compiler_params=pltpu.CompilerParams(
                 collective_id=0, has_side_effects=True, vmem_limit_bytes=32 * 1024 * 1024

time: 50 us -> 48.7 us (0.974)
  Pallas kernels: 45.3 us -> 43.9 us
    pallas_call x1, Pallas kernels: 45.3 us -> 43.9 us  [local(): pl.pallas_call(functools.partial(body, n_wide, n_narrow), out_shape=(shap...]
where the time goes in v2:
time: 48.7 us; the launch traced here: 48.5 us
  Pallas kernels  43.9 us (90%)
  local copies, waits for them, and re-layouts  3.88 us (8%)
  between operations  0.65 us (1%)
    pallas_call x1, Pallas kernels, local(): pl.pallas_call(functools.partial(body, n_wide, n_narrow), out_shape=(shap...  43.9 us
    unnamed x8, local copies, waits for them, and re-layouts  3.88 us

profile of v2, /device:TPU:0, one launch (start us, length us, event | category | flops | bytes accessed | tf_op | source)
XLA Modules:
  0.0 48.5 jit_solution(14555357332698087258)
XLA Ops:
  0.6 0.0 copy-start
  0.6 1.0 %copy-done = bf16[7,64,512]{2,1,0:T(8,128)(2,1)S(1)} copy-done((bf16[7,64,512]{2,1,0:T(8,128)(2,1)S(1)}, bf16[7,64,512]{2,1,0:T(8,128)(2,1)}, u32[]{:S(2)}) %copy-start) | copy-done | bytes 458776
  1.6 0.0 copy-start.1
  1.7 0.9 %copy-done.1 = f32[64,512]{1,0:T(8,128)S(1)} copy-done((f32[64,512]{1,0:T(8,128)S(1)}, f32[64,512]{1,0:T(8,128)}, u32[]{:S(2)}) %copy-start.1) | copy-done | bytes 131096
  2.6 0.0 copy-start.2
  2.6 0.7 %copy-done.2 = s32[1,1,64]{2,1,0:T(1,128)S(1)} copy-done((s32[1,1,64]{2,1,0:T(1,128)S(1)}, s32[1,1,64]{2,1,0:T(1,128)}, u32[]{:S(2)}) %copy-start.2) | copy-done | bytes 280
  3.2 43.9 %shard_map.50 = (f32[64,512]{1,0:T(8,128)S(1)}, f32[64,512]{1,0:T(8,128)S(1)}) custom-call(f32[64,512]{1,0:T(8,128)S(1)} %copy-done.1, bf16[7,64,512]{2,1,0:T(8,128)(2,1)S(1)} %copy-done, s32[1,1,64]{2,1,0:T(1,128)S(1)} %copy-done.2), custom_call_target="tpu_custom_call" | custom-call | tf_op jit(solution)/shard_map/pallas_call | solution.py:625
  47.2 0.7 %copy.7 = f32[64,512]{1,0:T(8,128)} copy(f32[64,512]{1,0:T(8,128)S(1)} %get-tuple-element.4) | data formatting | bytes 262144
  47.8 0.7 %copy.8 = f32[64,512]{1,0:T(8,128)} copy(f32[64,512]{1,0:T(8,128)S(1)} %get-tuple-element.5) | data formatting | bytes 262144
Async XLA Ops:
  0.6 1.0 %copy-start = (bf16[7,64,512]{2,1,0:T(8,128)(2,1)S(1)}, bf16[7,64,512]{2,1,0:T(8,128)(2,1)}, u32[]{:S(2)}) copy-start(bf16[7,64,512]{2,1,0:T(8,128)(2,1)} %geom_hbm.1) | copy-start | bytes 1376260
  1.6 0.9 %copy-start.1 = (f32[64,512]{1,0:T(8,128)S(1)}, f32[64,512]{1,0:T(8,128)}, u32[]{:S(2)}) copy-start(f32[64,512]{1,0:T(8,128)} %load_hbm.1) | copy-start | bytes 393220
  2.6 0.7 %copy-start.2 = (s32[1,1,64]{2,1,0:T(1,128)S(1)}, s32[1,1,64]{2,1,0:T(1,128)}, u32[]{:S(2)}) copy-start(s32[1,1,64]{2,1,0:T(1,128)} %order_hbm.1) | copy-start | bytes 772

commit v3 on v2

--- a/solution.py
+++ b/solution.py
@@ -263,23 +263,20 @@
     q_r = jnp.full((8, 128), float(ROW_TOTAL[0]), F32)
     for k in range(1, 4):
         q_r = jnp.where((node == k) | (node == 7 - k), float(ROW_TOTAL[k]), q_r)
-    h_z, part_a = [], []
-    for i in range(8):
+    h_z, part_a = [None] * 8, [None] * 8
+
+    def by_cycle(value):
+        return jnp.stack([value[j] * float(ROW_TOTAL[j]) for j in range(4)])
+
+    def bound_fluxes(i):
         a = [jnp.abs(slab(metric.at[q], i)) for q in range(6)]
         q_z = float(ROW_TOTAL[i])
-
-        def by_cycle(value):
-            return jnp.stack([value[j] * float(ROW_TOTAL[j]) for j in range(4)])
-
-        h_z.append(a[0] * q_z + by_cycle(a[3]) + a[4] * q_r)
-        part_a.append(along_mirrored(a[3] * q_z + by_cycle(a[1]) + a[5] * q_r, ABS.T, 1))
+        h_z[i] = a[0] * q_z + by_cycle(a[3]) + a[4] * q_r
+        part_a[i] = along_mirrored(a[3] * q_z + by_cycle(a[1]) + a[5] * q_r, ABS.T, 1)
         put(radial_in, i, a[4] * q_z + by_cycle(a[5]) + a[2] * q_r)
-    radial_apply(radial_in, ABS.T, 1)
-    part_z = along_eight(h_z, ABS.T, 1)
-    for i in range(8):
+
+    def bound_total(i, part_z):
         put(fields.at[1], i, part_z[i] + part_a[i] + slab(radial_out, i) + jnp.abs(slab(metric.at[6], i)))
-    for q in (3, 5):
-        metric[q] = metric[q] * mirror
 
     even, odd = halves(DERIV)
     even_t, odd_t = halves(DERIV.T)
@@ -479,10 +476,22 @@
         rhos.append(1.0 / (2.0 * sigma - rhos[-1]))
 
     assemble_own(0, 0, 32)
-    assemble_own(1, 0, 32)
+    for i in range(8):
+        bound_fluxes(i)
+    part_z = along_eight(h_z, ABS.T, 1)
+    radial_apply(radial_in, ABS.T, 1, 0, 8)
+    for i in FACE:
+        bound_total(i, part_z)
+    assemble_own(1, 0, 8)
     pl.semaphore_wait(barrier, len(greeted))
     pipe = send_pipe(1) + send_pipe(0)
+    radial_apply(radial_in, ABS.T, 1, 8, 24)
+    for i in INNER:
+        bound_total(i, part_z)
+    assemble_own(1, 8, 24)
     cycle = send_cycle(1) + send_cycle(0)
+    for q in (3, 5):
+        metric[q] = metric[q] * mirror
 
     def begin(i):
         inverse = 1.0 / whole_plane(1, i)
@@ -663,7 +672,7 @@
                 dma((3,)),
             ],
             compiler_params=pltpu.CompilerParams(
-                collective_id=0, has_side_effects=True, vmem_limit_bytes=32 * 1024 * 1024
+                collective_id=0, has_side_effects=True, vmem_limit_bytes=60 * 1024 * 1024
             ),
         )(load, geom, element_order)
 

time: 48.7 us -> 48 us (0.986)
  local copies, waits for them, and re-layouts: 3.88 us -> 2.26 us
  Pallas kernels: 43.9 us -> 44.9 us
    unnamed x8 -> x4, local copies, waits for them, and re-layouts: 3.88 us -> 2.26 us
    pallas_call x1, Pallas kernels: 43.9 us -> 44.9 us  [local(): pl.pallas_call(functools.partial(body, n_wide, n_narrow), out_shape=(shap...]
where the time goes in v3:
time: 48 us; the launch traced here: 47.8 us
  Pallas kernels  44.9 us (94%)
  local copies, waits for them, and re-layouts  2.26 us (5%)
  between operations  0.65 us (1%)
    pallas_call x1, Pallas kernels, local(): pl.pallas_call(functools.partial(body, n_wide, n_narrow), out_shape=(shap...  44.9 us
    unnamed x4, local copies, waits for them, and re-layouts  2.26 us

profile of v3, /device:TPU:0, one launch (start us, length us, event | category | flops | bytes accessed | tf_op | source)
XLA Modules:
  0.0 47.8 jit_solution(14701941506875583735)
XLA Ops:
  0.6 44.9 %shard_map.50 = (f32[64,512]{1,0:T(8,128)}, f32[64,512]{1,0:T(8,128)}) custom-call(f32[64,512]{1,0:T(8,128)} %load_hbm.1, bf16[7,64,512]{2,1,0:T(8,128)(2,1)} %geom_hbm.1, s32[1,1,64]{2,1,0:T(1,128)} %order_hbm.1), custom_call_target="tpu_custom_call" | custom-call | tf_op jit(solution)/shard_map/pallas_call | solution.py:634
  45.6 0.0 copy-start
  45.6 1.6 %copy.7 = f32[64,512]{1,0:T(8,128)} copy(f32[64,512]{1,0:T(8,128)} %get-tuple-element.4) | data formatting | bytes 262144
  47.2 0.0 copy-done
  47.2 0.7 %copy.8 = f32[64,512]{1,0:T(8,128)} copy(f32[64,512]{1,0:T(8,128)S(1)} %copy-done) | data formatting | bytes 262144
Async XLA Ops:
  45.6 1.6 %copy-start = (f32[64,512]{1,0:T(8,128)S(1)}, f32[64,512]{1,0:T(8,128)}, u32[]{:S(2)}) copy-start(f32[64,512]{1,0:T(8,128)} %get-tuple-element.5) | copy-start | bytes 393220

commit v4 on v3

--- a/solution.py
+++ b/solution.py
@@ -139,6 +139,10 @@
     grad_z,
     fields,
     faces,
+    far_plane,
+    far_line,
+    planes,
+    from_planes,
     res,
     binv,
     zed,
@@ -160,6 +164,8 @@
     g_send,
     g_recv,
     in_sem,
+    p_send,
+    p_recv,
 ):
     fetches = [
         pltpu.make_async_copy(order_hbm, order_ref, in_sem.at[0]),
@@ -170,8 +176,9 @@
         fetch.start()
     w = lax.axis_index("wide")
     n = lax.axis_index("narrow")
-    up = lax.rem(w + 1, n_wide)
-    down = lax.rem(w + n_wide - 1, n_wide)
+    odd_one = lax.rem(w, 2)
+    near = lax.rem(w + n_wide + 1 - 2 * odd_one, n_wide)
+    far = lax.rem(w + n_wide - 1 + 2 * odd_one, n_wide)
     if n_narrow == 2:
         sides = [(lax.rem(n + 1, 2), 0)]
     else:
@@ -193,9 +200,9 @@
         stride *= factor
 
     barrier = pltpu.get_barrier_semaphore()
-    greeted = [(up, n), (down, n)]
+    greeted = [(near, n), (far, n)]
     for side, _ in sides:
-        greeted += [(up, side), (down, side), (w, side)]
+        greeted += [(near, side), (far, side), (w, side)]
     for partners in phases:
         greeted += partners
     for device in greeted:
@@ -207,6 +214,8 @@
     lane_row = lax.broadcasted_iota(jnp.int32, (1, 128), 1)
     mirror = jnp.where(lane_row < 64, 1.0, -1.0).astype(F32)
     radial_row = lane_row % 16
+    odd_row = (lane_row * 0 + odd_one) == 1
+    pipe_mirror = jnp.where(odd_row, -1.0, 1.0).astype(F32)
 
     for fetch in fetches:
         fetch.wait()
@@ -224,6 +233,11 @@
         [jnp.concatenate([bottom, zero], axis=1), jnp.concatenate([zero, bottom], axis=1)], axis=0
     ).astype(jnp.bfloat16)
 
+    def oriented(value):
+        pairs = value.reshape(4, 2, 32, 128)
+        swapped = jnp.stack([pairs[:, 1], pairs[:, 0]], axis=1).reshape(256, 128)
+        return jnp.where(odd_row, swapped, value)
+
     def place_pair(one, two):
         turned = jnp.transpose(jnp.concatenate([one, two], axis=0)).astype(jnp.bfloat16)
         split = turned.reshape(8, 8, 8, 128)
@@ -231,7 +245,8 @@
         high = jnp.stack([split[i, 7 - j] for i in ORDER for j in range(4)]).reshape(256, 128)
         both = jnp.dot(low, into_low, preferred_element_type=F32)
         both = both + jnp.dot(high, into_high, preferred_element_type=F32)
-        return both[:, :128], both[:, 128:]
+        one, two = both[:, :128], both[:, 128:]
+        return oriented(one), oriented(two)
 
     def rounded(value):
         return value.astype(jnp.bfloat16).astype(F32)
@@ -304,42 +319,61 @@
     def put_tile(ref, i, j, value):
         ref[pl.ds(32 * POS[i] + 8 * j, 8), :] = value
 
-    def forward_face(f):
-        radial_apply(zed, DERIV, -1, 0, 8)
-        grad_a = {i: along_mirrored(slab(zed, i), DERIV, 1) for i in FACE}
-        energy = jnp.zeros((8, 128), F32)
-        flux_a = {i: [] for i in FACE}
-        pieces = {i: [] for i in FACE}
-        for j in range(4):
-            v0, v7 = tile(zed, 0, j), tile(zed, 7, j)
-            plus, minus = v0 + v7, v0 - v7
-            flux_z = [None] * 8
-            for i in range(4):
-                e, o = plus * float(even[i][0]), minus * float(odd[i][0])
-                for node_i, extra in ((i, e + o), (7 - i, o - e)):
-                    slope = tile(grad_z, node_i, j) + extra
-                    put_tile(grad_z, node_i, j, slope)
-                    if node_i in FACE:
-                        g = [tile(metric.at[q], node_i, j) for q in range(6)]
-                        slope_a = grad_a[node_i][j]
-                        slope_r = tile(radial_out, node_i, j)
-                        flux = g[0] * slope + g[3] * slope_a + g[4] * slope_r
-                        flux_a[node_i].append(g[3] * slope + g[1] * slope_a + g[5] * slope_r)
-                        put_tile(radial_in, node_i, j, g[4] * slope + g[5] * slope_a + g[2] * slope_r)
-                    else:
-                        flux = tile(part_fz, node_i, j) + tile(metric.at[0], node_i, j) * slope
-                    put_tile(part_fz, node_i, j, flux)
-                    flux_z[node_i] = flux
-            e = combine(even_t[0], [flux_z[m] + flux_z[7 - m] for m in range(4)])
-            o = combine(odd_t[0], [flux_z[m] - flux_z[7 - m] for m in range(4)])
-            pieces[0].append(e + o + tile(metric.at[6], 0, j) * v0)
-            pieces[7].append(o - e + tile(metric.at[6], 7, j) * v7)
+    def add_slopes(column, plane):
+        for i in range(8):
+            put(grad_z, i, slab(grad_z, i) + plane * float(DERIV[i][column]))
+
+    def forward_far(f):
+        radial_apply(zed, DERIV, -1, 4, 4)
+        plane = slab(zed, 7)
+        grad_a = along_mirrored(plane, DERIV, 1)
+        grad_r = slab(radial_out, 7)
+        add_slopes(7, plane)
+        put(part_fz, 7, slab(metric.at[3], 7) * grad_a + slab(metric.at[4], 7) * grad_r)
+        put(part_fa, 7, slab(metric.at[1], 7) * grad_a + slab(metric.at[5], 7) * grad_r)
+        put(part_fr, 7, slab(metric.at[5], 7) * grad_a + slab(metric.at[2], 7) * grad_r)
+        slope = slab(grad_z, 0)
+        put(radial_in, 0, slab(metric.at[4], 0) * slope)
+        radial_apply(radial_in, DERIV.T, -1, 0, 4)
+        total = along_mirrored(slab(metric.at[3], 0) * slope, DERIV.T, -1) + slab(metric.at[0], 0) * slope * float(DERIV[0][0])
+        for i in range(1, 8):
+            flux = slab(part_fz, i) + slab(metric.at[0], i) * slab(grad_z, i)
+            total = total + flux * float(DERIV[i][0])
+        total = total + slab(radial_out, 0)
+        far_plane[f] = total.reshape(32, 128)
+
+        def keep(at, s, message):
+            far_line[f, s] = message
+
+        assemble_at(far_plane.at[f], 0, 4, keep)
+        copies = [send(far_plane.at[f], from_z.at[f, 0], z_send.at[f, 0], z_recv.at[f, 0], (far, n))]
+        for s, (side, _) in enumerate(sides):
+            copies.append(send(far_line.at[f, s], from_c.at[f, s, 0], c_send.at[f, s, 0], c_recv.at[f, s, 0], (far, side)))
+        return total, copies
+
+    def forward_face(f, far_part):
+        radial_apply(zed, DERIV, -1, 0, 4)
+        plane = slab(zed, 0)
+        grad_a = along_mirrored(plane, DERIV, 1)
+        grad_r = slab(radial_out, 0)
+        add_slopes(0, plane)
+        c = [planes[q].reshape(4, 8, 128) for q in range(6)]
+        put(radial_in, 0, c[2] * plane + c[5] * grad_a + c[4] * grad_r)
+        flux_a = c[1] * plane + c[3] * grad_a + c[5] * grad_r
+        put(part_fz, 0, slab(metric.at[3], 0) * grad_a + slab(metric.at[4], 0) * grad_r)
+        near_slope = slab(grad_z, 7)
+        put(radial_in, 7, slab(part_fr, 7) + slab(metric.at[4], 7) * near_slope)
         radial_apply(radial_in, DERIV.T, -1, 0, 8)
-        for i in FACE:
-            total = jnp.stack(pieces[i]) + along_mirrored(jnp.stack(flux_a[i]), DERIV.T, -1) + slab(radial_out, i)
-            put(fields.at[f], i, total)
-            energy = energy + jnp.sum(total * slab(zed, i), axis=0)
-        return energy
+        own = c[0] * plane + c[1] * grad_a + c[2] * grad_r + along_mirrored(flux_a, DERIV.T, -1) + slab(radial_out, 0)
+        total = along_mirrored(slab(part_fa, 7) + slab(metric.at[3], 7) * near_slope, DERIV.T, -1)
+        total = total + slab(metric.at[6], 7) * slab(zed, 7) + slab(radial_out, 7)
+        for i in range(8):
+            flux = slab(part_fz, i) + slab(metric.at[0], i) * slab(grad_z, i)
+            put(part_fz, i, flux)
+            total = total + flux * float(DERIV[i][7])
+        put(fields.at[f], 0, own + far_part)
+        put(fields.at[f], 7, total)
+        return jnp.sum((far_part + own * 0.5) * plane + total * slab(zed, 7), axis=0)
 
     def forward_rest(f):
         energy = jnp.zeros((8, 128), F32)
@@ -362,7 +396,12 @@
         return energy
 
     def assemble_own(f, start, count):
-        ref = fields.at[f]
+        def keep(at, s, message):
+            faces[f, s, pl.ds(8 * at, 8), :] = message
+
+        assemble_at(fields.at[f], start, count, keep)
+
+    def assemble_at(ref, start, count, keep):
         low = pl.ds(8 * start, count, stride=8)
         high = pl.ds(8 * start + 7, count, stride=8)
         inner, outer = ref[low, :], ref[high, :]
@@ -378,7 +417,7 @@
                     message = jnp.where(lane < 16, below, message)
                 if kind in (0, 2):
                     message = jnp.where(lane >= 112, above, message)
-                faces[f, s, pl.ds(8 * at, 8), :] = message
+                keep(at, s, message)
             inside = jnp.where(lane < 64, pltpu.roll(row, 80, 1), pltpu.roll(row, 48, 1))
             ref[pl.ds(32 * at, 8), :] = row + jnp.where((lane >= 16) & (lane < 112), inside, 0.0)
 
@@ -392,16 +431,15 @@
         started.append(copy)
         return copy
 
-    def send_pipe(f):
+    def send_face(f, face, device):
+        rows, line = pl.ds(32 * face, 32), pl.ds(8 * face, 8)
         copies = [
-            send(fields.at[f, pl.ds(0, 32)], from_z.at[f, 1], z_send.at[f, 1], z_recv.at[f, 1], (down, n)),
-            send(fields.at[f, pl.ds(32, 32)], from_z.at[f, 0], z_send.at[f, 0], z_recv.at[f, 0], (up, n)),
+            send(fields.at[f, rows], from_z.at[f, face], z_send.at[f, face], z_recv.at[f, face], (device, n))
         ]
         for s, (side, _) in enumerate(sides):
-            copies += [
-                send(faces.at[f, s, pl.ds(0, 8)], from_c.at[f, s, 1], c_send.at[f, s, 1], c_recv.at[f, s, 1], (down, side)),
-                send(faces.at[f, s, pl.ds(8, 8)], from_c.at[f, s, 0], c_send.at[f, s, 0], c_recv.at[f, s, 0], (up, side)),
-            ]
+            copies.append(
+                send(faces.at[f, s, line], from_c.at[f, s, face], c_send.at[f, s, face], c_recv.at[f, s, face], (device, side))
+            )
         return copies
 
     def send_cycle(f):
@@ -484,14 +522,40 @@
         bound_total(i, part_z)
     assemble_own(1, 0, 8)
     pl.semaphore_wait(barrier, len(greeted))
-    pipe = send_pipe(1) + send_pipe(0)
+    from_far = send_face(1, 0, far) + send_face(0, 0, far)
+    from_near = send_face(1, 1, near) + send_face(0, 1, near)
+    corner = float(DERIV[0][0])
+    own = slab(metric.at[6], 0)
+    for i in range(8):
+        own = own + slab(metric.at[0], i) * float(DERIV[i][0] ** 2)
+    for q, plane in enumerate(
+        (
+            own,
+            slab(metric.at[3], 0) * (mirror * pipe_mirror * corner),
+            slab(metric.at[4], 0) * (pipe_mirror * corner),
+            slab(metric.at[1], 0),
+            slab(metric.at[2], 0),
+            slab(metric.at[5], 0) * mirror,
+        )
+    ):
+        planes[q] = plane.reshape(32, 128)
+    planes_copy = pltpu.make_async_remote_copy(
+        src_ref=planes,
+        dst_ref=from_planes,
+        send_sem=p_send.at[0],
+        recv_sem=p_recv.at[0],
+        device_id=(far, n),
+        device_id_type=MESH,
+    )
+    planes_copy.start()
     radial_apply(radial_in, ABS.T, 1, 8, 24)
     for i in INNER:
         bound_total(i, part_z)
     assemble_own(1, 8, 24)
     cycle = send_cycle(1) + send_cycle(0)
-    for q in (3, 5):
-        metric[q] = metric[q] * mirror
+    metric[3] = metric[3] * (mirror * pipe_mirror)
+    metric[4] = metric[4] * pipe_mirror
+    metric[5] = metric[5] * mirror
 
     def begin(i):
         inverse = 1.0 / whole_plane(1, i)
@@ -506,14 +570,23 @@
     for i in INNER:
         begin(i)
     forward_inner()
-    wait_all(pipe)
-    for i in FACE:
-        begin(i)
-
-    def apply_then(f, update, between=None, last=None):
-        energy = forward_face(f)
+    wait_all(from_near)
+    begin(7)
+    pending = [from_far, lambda: begin(0)]
+
+    def both_faces(f):
+        far_part, copies = forward_far(f)
+        wait_all(pending[0])
+        pending[1]()
+        if f == 2:
+            planes_copy.wait()
+            planes[...] = planes[...] + from_planes[...]
+        energy = forward_face(f, far_part)
         assemble_own(f, 0, 8)
-        pipe = send_pipe(f)
+        return energy, copies, send_face(f, 1, near)
+
+    def apply_then(f, update, between=None):
+        energy, from_far, from_near = both_faces(f)
         energy = energy + forward_rest(f)
         assemble_own(f, 8, 24)
         cycle = send_cycle(f)
@@ -522,9 +595,9 @@
         for i in INNER:
             update(i, whole_plane(f, i))
         forward_inner()
-        wait_all(pipe)
-        for i in FACE:
-            update(i, whole_plane(f, i))
+        wait_all(from_near)
+        update(7, whole_plane(f, 7))
+        pending[:] = [from_far, lambda: update(0, whole_plane(f, 0))]
         return after
 
     def smoothed(source, step, i, plane):
@@ -570,14 +643,14 @@
     apply_then(6, step_on, finish_norm)
     norm_0, energy_0, alpha_0 = scalars["norm"], scalars["energy"], scalars["alpha"]
 
-    def read_back(value_of, planes):
+    def read_back(value_of, chosen):
         rows = []
-        for i in planes:
-            value = value_of(i)
+        for i in chosen:
+            value = jnp.where(odd_row, value_of(7 - i), value_of(i))
             for j in range(8):
                 keep = (lane < 64) if j < 4 else (lane >= 64)
                 rows.append(jnp.where(keep, value[j if j < 4 else 7 - j], 0.0))
-        full = jnp.stack(rows).reshape(64 * len(planes), 128)
+        full = jnp.stack(rows).reshape(64 * len(chosen), 128)
         high = full.astype(jnp.bfloat16)
         low = (full - high.astype(F32)).astype(jnp.bfloat16)
         dims = (((1,), (1,)), ((), ()))
@@ -585,9 +658,7 @@
             hot_both, low, dims, preferred_element_type=F32
         )
 
-    energy = forward_face(7)
-    assemble_own(7, 0, 8)
-    pipe = send_pipe(7)
+    energy, from_far, from_near = both_faces(7)
     energy = energy + forward_rest(7)
     norm = weighted(lambda i: slab(res, i), lambda i: slab(zed, i))
     cross = weighted(lambda i: slab(zed, i), lambda i: slab(image, i))
@@ -611,7 +682,8 @@
     solution_ref[...] = (alpha_0 + alpha_1 * beta) * read[0] + alpha_1 * read[1]
     residual = read[2] - (alpha_1 * beta) * read[3]
     residual_ref[:, 128:384] = residual[:, 128:384] - alpha_1 * middle
-    wait_all(pipe)
+    wait_all(from_near)
+    wait_all(from_far)
     ends = read_back(lambda i: whole_plane(7, i), (0, 1, 6, 7))
     residual_ref[:, 0:128] = residual[:, 0:128] - alpha_1 * ends[:, 0:128]
     residual_ref[:, 384:512] = residual[:, 384:512] - alpha_1 * ends[:, 128:256]
@@ -649,6 +721,10 @@
                 block,
                 vmem((FIELDS, 256, 128), F32),
                 vmem((FIELDS, sides, 64, 128), F32),
+                vmem((FIELDS, 32, 128), F32),
+                vmem((FIELDS, sides, 8, 128), F32),
+                vmem((6, 32, 128), F32),
+                vmem((6, 32, 128), F32),
                 block,
                 block,
                 block,
@@ -670,6 +746,8 @@
                 dma((2, partners)),
                 dma((2, partners)),
                 dma((3,)),
+                dma((1,)),
+                dma((1,)),
             ],
             compiler_params=pltpu.CompilerParams(
                 collective_id=0, has_side_effects=True, vmem_limit_bytes=60 * 1024 * 1024

time: 48 us -> 44.1 us (0.919)
  Pallas kernels: 44.9 us -> 41 us
    pallas_call x1, Pallas kernels: 44.9 us -> 41 us  [local(): pl.pallas_call(functools.partial(body, n_wide, n_narrow), out_shape=(shap...]
where the time goes in v4:
time: 44.1 us; the launch traced here: 43.9 us
  Pallas kernels  41 us (93%)
  local copies, waits for them, and re-layouts  2.26 us (5%)
  between operations  0.65 us (1%)
    pallas_call x1, Pallas kernels, local(): pl.pallas_call(functools.partial(body, n_wide, n_narrow), out_shape=(shap...  41 us
    unnamed x4, local copies, waits for them, and re-layouts  2.26 us

profile of v4, /device:TPU:0, one launch (start us, length us, event | category | flops | bytes accessed | tf_op | source)
XLA Modules:
  0.0 43.9 jit_solution(2483973923597030047)
XLA Ops:
  0.6 41.0 %shard_map.50 = (f32[64,512]{1,0:T(8,128)}, f32[64,512]{1,0:T(8,128)}) custom-call(f32[64,512]{1,0:T(8,128)} %load_hbm.1, bf16[7,64,512]{2,1,0:T(8,128)(2,1)} %geom_hbm.1, s32[1,1,64]{2,1,0:T(1,128)} %order_hbm.1), custom_call_target="tpu_custom_call" | custom-call | tf_op jit(solution)/shard_map/pallas_call | solution.py:706
  41.6 0.0 copy-start
  41.6 1.6 %copy.7 = f32[64,512]{1,0:T(8,128)} copy(f32[64,512]{1,0:T(8,128)} %get-tuple-element.4) | data formatting | bytes 262144
  43.2 0.0 copy-done
  43.3 0.7 %copy.8 = f32[64,512]{1,0:T(8,128)} copy(f32[64,512]{1,0:T(8,128)S(1)} %copy-done) | data formatting | bytes 262144
Async XLA Ops:
  41.6 1.6 %copy-start = (f32[64,512]{1,0:T(8,128)S(1)}, f32[64,512]{1,0:T(8,128)}, u32[]{:S(2)}) copy-start(f32[64,512]{1,0:T(8,128)} %get-tuple-element.5) | copy-start | bytes 393220

commit v5 on v4

--- a/solution.py
+++ b/solution.py
@@ -217,8 +217,8 @@
     odd_row = (lane_row * 0 + odd_one) == 1
     pipe_mirror = jnp.where(odd_row, -1.0, 1.0).astype(F32)
 
-    for fetch in fetches:
-        fetch.wait()
+    fetches[0].wait()
+    fetches[1].wait()
     order = order_ref[0].astype(jnp.int32)
     order_twice = jnp.concatenate([order, order + 64], axis=1)
     hot_t = (lax.broadcasted_iota(jnp.int32, (128, 128), 0) == order_twice).astype(F32)
@@ -239,24 +239,25 @@
         return jnp.where(odd_row, swapped, value)
 
     def place_pair(one, two):
-        turned = jnp.transpose(jnp.concatenate([one, two], axis=0)).astype(jnp.bfloat16)
+        turned = jnp.transpose(jnp.concatenate([one, two], axis=0)).astype(F32)
         split = turned.reshape(8, 8, 8, 128)
-        low = jnp.stack([split[i, j] for i in ORDER for j in range(4)]).reshape(256, 128)
-        high = jnp.stack([split[i, 7 - j] for i in ORDER for j in range(4)]).reshape(256, 128)
+        low = jnp.stack([split[i, j] for i in ORDER for j in range(4)]).reshape(256, 128).astype(jnp.bfloat16)
+        high = jnp.stack([split[i, 7 - j] for i in ORDER for j in range(4)]).reshape(256, 128).astype(jnp.bfloat16)
         both = jnp.dot(low, into_low, preferred_element_type=F32)
         both = both + jnp.dot(high, into_high, preferred_element_type=F32)
         one, two = both[:, :128], both[:, 128:]
         return oriented(one), oriented(two)
 
     def rounded(value):
-        return value.astype(jnp.bfloat16).astype(F32)
+        return value.astype(jnp.bfloat16)
 
     load = load_ref[...]
     load_high = rounded(load)
-    load_rest = load - load_high
+    load_rest = load - load_high.astype(F32)
     load_mid = rounded(load_rest)
-    load_low = rounded(load_rest - load_mid)
-    g = [geom_ref[q].astype(F32) for q in range(7)]
+    load_low = rounded(load_rest - load_mid.astype(F32))
+    fetches[2].wait()
+    g = [geom_ref[q] for q in range(7)]
     for q in (0, 2, 4):
         metric[q], metric[q + 1] = place_pair(g[q], g[q + 1])
     metric[6], grid_high = place_pair(g[6], load_high)
@@ -465,9 +466,9 @@
         for copy in copies:
             copy.wait_recv()
 
-    def weighted(one, two):
+    def weighted(one, two, chosen=range(8)):
         total = None
-        for i in range(8):
+        for i in chosen:
             product = one(i) * two(i)
             term = (product[1] + product[2]) + product[3] + product[0] * 0.5
             if i in (0, 7):
@@ -574,8 +575,10 @@
     begin(7)
     pending = [from_far, lambda: begin(0)]
 
-    def both_faces(f):
+    def both_faces(f, meanwhile=None):
         far_part, copies = forward_far(f)
+        if meanwhile is not None:
+            meanwhile()
         wait_all(pending[0])
         pending[1]()
         if f == 2:
@@ -585,8 +588,8 @@
         assemble_own(f, 0, 8)
         return energy, copies, send_face(f, 1, near)
 
-    def apply_then(f, update, between=None):
-        energy, from_far, from_near = both_faces(f)
+    def apply_then(f, update, between=None, meanwhile=None):
+        energy, from_far, from_near = both_faces(f, meanwhile)
         energy = energy + forward_rest(f)
         assemble_own(f, 8, 24)
         cycle = send_cycle(f)
@@ -639,9 +642,6 @@
         end = slab(zed, i) + smoothed(image, 1, i, plane)
         put(res, i, slab(res, i) - scalars["alpha"] * slab(image, i))
         put(zed, i, slab(first, i) - scalars["alpha"] * end)
-
-    apply_then(6, step_on, finish_norm)
-    norm_0, energy_0, alpha_0 = scalars["norm"], scalars["energy"], scalars["alpha"]
 
     def read_back(value_of, chosen):
         rows = []
@@ -658,21 +658,37 @@
             hot_both, low, dims, preferred_element_type=F32
         )
 
-    energy, from_far, from_near = both_faces(7)
+    def read_first():
+        read[0] = read_back(lambda i: slab(first, i), range(8))
+
+    apply_then(6, step_on, finish_norm, read_first)
+    norm_0, energy_0, alpha_0 = scalars["norm"], scalars["energy"], scalars["alpha"]
+
+    sums_of = {}
+
+    def norm_and_cross(chosen):
+        return (
+            weighted(lambda i: slab(res, i), lambda i: slab(zed, i), chosen),
+            weighted(lambda i: slab(zed, i), lambda i: slab(image, i), chosen),
+        )
+
+    def prepare():
+        sums_of["norm"], sums_of["cross"] = norm_and_cross(range(1, 8))
+        read[3] = read_back(lambda i: slab(image, i), range(8))
+
+    energy, from_far, from_near = both_faces(7, prepare)
+    norm, cross = norm_and_cross([0])
+    norm, cross = norm + sums_of["norm"], cross + sums_of["cross"]
     energy = energy + forward_rest(7)
-    norm = weighted(lambda i: slab(res, i), lambda i: slab(zed, i))
-    cross = weighted(lambda i: slab(zed, i), lambda i: slab(image, i))
     sums = sum_start(1, 0, stack_rows([norm, cross, energy]))
     assemble_own(7, 8, 24)
     cycle = send_cycle(7)
-    for q, ref in enumerate((first, zed)):
-        read[q] = read_back(lambda i: slab(ref, i), range(8))
+    read[1] = read_back(lambda i: slab(zed, i), range(8))
     totals = sum_end(1, 0, sums)
     for later in range(1, len(phases) - 1):
         totals = sum_end(1, later, sum_start(1, later, totals))
     sums = sum_start(1, len(phases) - 1, totals)
-    for q, ref in enumerate((res, image)):
-        read[2 + q] = read_back(lambda i: slab(ref, i), range(8))
+    read[2] = read_back(lambda i: slab(res, i), range(8))
     wait_all(cycle)
     middle = read_back(lambda i: whole_plane(7, i), range(2, 6))
     total = jnp.sum(sum_end(1, len(phases) - 1, sums), axis=1, keepdims=True)

time: 44.1 us -> 43.9 us (level)
  no operation moved by 1% of the time
where the time goes in v5:
time: 43.9 us; the launch traced here: 43.8 us
  Pallas kernels  40.9 us (93%)
  local copies, waits for them, and re-layouts  2.26 us (5%)
  between operations  0.65 us (1%)
    pallas_call x1, Pallas kernels, local(): pl.pallas_call(functools.partial(body, n_wide, n_narrow), out_shape=(shap...  40.9 us
    unnamed x4, local copies, waits for them, and re-layouts  2.26 us

profile of v5, /device:TPU:0, one launch (start us, length us, event | category | flops | bytes accessed | tf_op | source)
XLA Modules:
  0.0 43.8 jit_solution(11945656101650151223)
XLA Ops:
  0.6 40.9 %shard_map.50 = (f32[64,512]{1,0:T(8,128)}, f32[64,512]{1,0:T(8,128)}) custom-call(f32[64,512]{1,0:T(8,128)} %load_hbm.1, bf16[7,64,512]{2,1,0:T(8,128)(2,1)} %geom_hbm.1, s32[1,1,64]{2,1,0:T(1,128)} %order_hbm.1), custom_call_target="tpu_custom_call" | custom-call | tf_op jit(solution)/shard_map/pallas_call | solution.py:722
  41.5 0.0 copy-start
  41.5 1.6 %copy.7 = f32[64,512]{1,0:T(8,128)} copy(f32[64,512]{1,0:T(8,128)} %get-tuple-element.4) | data formatting | bytes 262144
  43.1 0.0 copy-done
  43.1 0.7 %copy.8 = f32[64,512]{1,0:T(8,128)} copy(f32[64,512]{1,0:T(8,128)S(1)} %copy-done) | data formatting | bytes 262144
Async XLA Ops:
  41.5 1.6 %copy-start = (f32[64,512]{1,0:T(8,128)S(1)}, f32[64,512]{1,0:T(8,128)}, u32[]{:S(2)}) copy-start(f32[64,512]{1,0:T(8,128)} %get-tuple-element.5) | copy-start | bytes 393220

commit v6 on v5

--- a/solution.py
+++ b/solution.py
@@ -384,7 +384,10 @@
             put(radial_in, i, slab(part_fr, i) + slab(metric.at[4], i) * slope)
             put(part_fa, i, along_mirrored(flux_a, DERIV.T, -1) + slab(metric.at[6], i) * slab(zed, i))
         radial_apply(radial_in, DERIV.T, -1, 8, 24)
+        copies = None
         for j in range(4):
+            if j == 1:
+                copies = send_edges(f)
             flux_z = [tile(part_fz, i, j) for i in range(8)]
             sums = [flux_z[m] + flux_z[7 - m] for m in range(4)]
             differences = [flux_z[m] - flux_z[7 - m] for m in range(4)]
@@ -394,11 +397,33 @@
                     total = piece + tile(part_fa, node_i, j) + tile(radial_out, node_i, j)
                     put_tile(fields.at[f], node_i, j, total)
                     energy = energy + total * tile(zed, node_i, j)
-        return energy
+        return energy, copies
+
+    def send_edges(f):
+        for i in INNER:
+            row = tile(fields.at[f], i, 0)
+            down_one = pltpu.roll(pltpu.roll(row, 1, 0), 1, 1)
+            up_one = pltpu.roll(pltpu.roll(row, 7, 0), 127, 1)
+            row = row + jnp.where((node == 0) & (radial > 0), down_one, 0.0)
+            row = row + jnp.where((node == 7) & (radial < 15), up_one, 0.0)
+            keep_line(f, POS[i], row)
+        return send_cycle(f)
+
+    def keep_line(f, at, row):
+        below = pltpu.roll(row, 16, 1)
+        above = pltpu.roll(row, 112, 1)
+        for s, (_, kind) in enumerate(sides):
+            message = jnp.zeros_like(row)
+            if kind in (0, 1):
+                message = jnp.where(lane < 16, below, message)
+            if kind in (0, 2):
+                message = jnp.where(lane >= 112, above, message)
+            faces[f, s, pl.ds(8 * at, 8), :] = message
 
     def assemble_own(f, start, count):
         def keep(at, s, message):
-            faces[f, s, pl.ds(8 * at, 8), :] = message
+            if f < 2 or at < 2:
+                faces[f, s, pl.ds(8 * at, 8), :] = message
 
         assemble_at(fields.at[f], start, count, keep)
 
@@ -590,9 +615,9 @@
 
     def apply_then(f, update, between=None, meanwhile=None):
         energy, from_far, from_near = both_faces(f, meanwhile)
-        energy = energy + forward_rest(f)
+        more, cycle = forward_rest(f)
+        energy = energy + more
         assemble_own(f, 8, 24)
-        cycle = send_cycle(f)
         after = between(energy) if between is not None else None
         wait_all(cycle)
         for i in INNER:
@@ -679,10 +704,10 @@
     energy, from_far, from_near = both_faces(7, prepare)
     norm, cross = norm_and_cross([0])
     norm, cross = norm + sums_of["norm"], cross + sums_of["cross"]
-    energy = energy + forward_rest(7)
+    more, cycle = forward_rest(7)
+    energy = energy + more
     sums = sum_start(1, 0, stack_rows([norm, cross, energy]))
     assemble_own(7, 8, 24)
-    cycle = send_cycle(7)
     read[1] = read_back(lambda i: slab(zed, i), range(8))
     totals = sum_end(1, 0, sums)
     for later in range(1, len(phases) - 1):

time: 43.9 us -> 44 us (level)
  no operation moved by 1% of the time
where the time goes in v6:
time: 44 us; the launch traced here: 43.8 us
  Pallas kernels  40.9 us (93%)
  local copies, waits for them, and re-layouts  2.26 us (5%)
  between operations  0.65 us (1%)
    pallas_call x1, Pallas kernels, local(): pl.pallas_call(functools.partial(body, n_wide, n_narrow), out_shape=(shap...  40.9 us
    unnamed x4, local copies, waits for them, and re-layouts  2.26 us

profile of v6, /device:TPU:0, one launch (start us, length us, event | category | flops | bytes accessed | tf_op | source)
XLA Modules:
  0.0 43.8 jit_solution(2769917732522736968)
XLA Ops:
  0.6 40.9 %shard_map.50 = (f32[64,512]{1,0:T(8,128)}, f32[64,512]{1,0:T(8,128)}) custom-call(f32[64,512]{1,0:T(8,128)} %load_hbm.1, bf16[7,64,512]{2,1,0:T(8,128)(2,1)} %geom_hbm.1, s32[1,1,64]{2,1,0:T(1,128)} %order_hbm.1), custom_call_target="tpu_custom_call" | custom-call | tf_op jit(solution)/shard_map/pallas_call | solution.py:747
  41.5 0.0 copy-start
  41.5 1.6 %copy.7 = f32[64,512]{1,0:T(8,128)} copy(f32[64,512]{1,0:T(8,128)} %get-tuple-element.4) | data formatting | bytes 262144
  43.1 0.0 copy-done
  43.1 0.7 %copy.8 = f32[64,512]{1,0:T(8,128)} copy(f32[64,512]{1,0:T(8,128)S(1)} %copy-done) | data formatting | bytes 262144
Async XLA Ops:
  41.5 1.6 %copy-start = (f32[64,512]{1,0:T(8,128)S(1)}, f32[64,512]{1,0:T(8,128)}, u32[]{:S(2)}) copy-start(f32[64,512]{1,0:T(8,128)} %get-tuple-element.5) | copy-start | bytes 393220
